TPU v7x, 32 devices: a whole 2x2x4 slice. The times are simulated.
32 devices in a mesh: dp: 8 (over z, x), fsdp: 4 (over y, core).
Axes of the slice: x: 2, y: 2, z: 4, core: 2. Of those that a mesh axis runs over, the one named last changes fastest.
Arguments:
- tokens: bfloat16 [16384, 768], P(('dp', 'fsdp')), may hold values from -6 to 6
- attn_gain: bfloat16 [768], P(('dp', 'fsdp')), may hold values from 0.5 to 1.5
- qkv_weight: bfloat16 [768, 2304], P(('dp', 'fsdp')), may hold values from -0.109375 to 0.109375
- out_weight: bfloat16 [768, 768], P(('dp', 'fsdp')), may hold values from -1.75 to 1.75
- ffn_gain: bfloat16 [768], P(('dp', 'fsdp')), may hold values from 0.5 to 1.5
- router_weight: bfloat16 [768, 2], P(('dp', 'fsdp')), may hold values from -0.15625 to 0.15625
- inner_weight: bfloat16 [2, 768, 6144], P(None, ('dp', 'fsdp')), may hold values from -0.21875 to 0.21875
- outer_weight: bfloat16 [2, 3072, 768], P(None, ('dp', 'fsdp')), may hold values from -0.3125 to 0.3125
- bias_table: float32 [32, 12], replicated, may hold values from -5 to 5
- lengths: int32 [32, 4], P(('dp', 'fsdp')), may hold values from 0 to 512, as said below
- routes: int32 [16384, 1], P(('dp', 'fsdp')), may hold values from 0 to 1; in each aligned block of 512 rows (0 to 511, 512 to 1023, ...) at most 320 rows name the same one
- buckets: int32 [1023], replicated, may hold values from 0 to 31, as said below
- out_cotangent: bfloat16 [16384, 768], P(('dp', 'fsdp')), may hold values from -6 to 6
Outputs:
- mixed: bfloat16 [16384, 768], P(('dp', 'fsdp'))
- tokens_grad: float32 [16384, 768], P(('dp', 'fsdp'))
- attn_gain_grad: float32 [768], P(('dp', 'fsdp'))
- qkv_weight_grad: float32 [768, 2304], P(('dp', 'fsdp'))
- out_weight_grad: float32 [768, 768], P(('dp', 'fsdp'))
- ffn_gain_grad: float32 [768], P(('dp', 'fsdp'))
- router_grad: float32 [768, 2], P(('dp', 'fsdp'))
- inner_grad: float32 [2, 768, 6144], P(None, ('dp', 'fsdp'))
- outer_grad: float32 [2, 3072, 768], P(None, ('dp', 'fsdp'))
- table_grad: float32 [32, 12], replicated
Inputs may be any that keep to these rules, and one draw needn't show every extreme that they name: `lengths`: each row sums to at least 256 and at most 512; a length may be 0. In every draw some row holds a single sequence of 512 tokens. `routes`: among the rows of one device no expert is named by more than 320 rows, a bound that some block reaches. Entry o is the bucket of relative offset o - 511; buckets 0 to 15 serve offsets 0 and below, the rest positive offsets, and on either side the bucket does not fall as the distance grows.
All inputs are finite; a program needn't handle non-finite values.
Results may differ from a plain program's by a relative error of at most 0.015.
The roundings to bfloat16 on the way count: a program that leaves them out, or rounds other values in their place, can miss the bound.
Values may be sent and summed in bfloat16 or wider, within the bound.
A program may use at most 256 MiB of HBM per device.

v0:
```python
from functools import partial

import jax
import jax.numpy as jnp
from jax import lax
from jax.sharding import PartitionSpec as P

CAP = 320


EPSILON = 1e-06
NEGATIVE = -1e30
HIGHEST = lax.Precision.HIGHEST


def rms_scale(values, gain_row):
    return (
        values * lax.rsqrt(jnp.mean(values * values, axis=-1, keepdims=True) + EPSILON) * gain_row
    )


def gated_unit(gate_up):
    hidden_units = gate_up.shape[-1] // 2
    return jax.nn.gelu(gate_up[..., :hidden_units], approximate=True) * gate_up[..., hidden_units:]


def contract_rows(left_side, right_side):
    return lax.dot_general(
        left_side, right_side, (((0,), (0,)), ((), ())), preferred_element_type=jnp.float32
    )


def contract_cols(left_side, right_side):
    return lax.dot_general(
        left_side, right_side, (((1,), (1,)), ((), ())), preferred_element_type=jnp.float32
    )


def spread_offsets(offset_rows, first_row, block_rows, key_count):
    lane_count = offset_rows.shape[0]
    window = key_count + block_rows - 1
    padded = jnp.concatenate([offset_rows, jnp.zeros((lane_count, 1), jnp.float32)], axis=1)
    repeated = jnp.tile(padded, (1, block_rows))
    shifted = repeated[:, block_rows - 1 : block_rows - 1 + block_rows * window]
    return shifted.reshape(lane_count, block_rows, window)[:, :, :key_count]


def group_slices(projected, group_id, head_dim):
    model_width = projected.shape[1] // 3
    lane_count = 2 * head_dim
    query_cols = lax.dynamic_slice_in_dim(projected, group_id * lane_count, lane_count, 1)
    key_cols = lax.dynamic_slice_in_dim(
        projected, model_width + group_id * lane_count, lane_count, 1
    )
    value_cols = lax.dynamic_slice_in_dim(
        projected, 2 * model_width + group_id * lane_count, lane_count, 1
    )
    return (query_cols, key_cols, value_cols)


def masked_scores(query_split, key_split, bias_block, segment, first_row):
    block_rows = query_split.shape[0]
    scores = (
        jnp.einsum("qhd,khd->hqk", query_split, key_split, preferred_element_type=jnp.float32)
        + bias_block
    )
    same_doc = segment[first_row : first_row + block_rows, None] == segment[None, :]
    return jnp.where(same_doc[None], scores, NEGATIVE)


def attend_forward(projected, offset_rows, segment, group_id, head_dim, block_rows):
    row_count = projected.shape[0]
    lane_count = 2 * head_dim
    query_cols, key_cols, value_cols = group_slices(projected, group_id, head_dim)
    key_split = key_cols.reshape(row_count, 2, head_dim)
    value_split = value_cols.reshape(row_count, 2, head_dim)
    offset_group = lax.dynamic_slice_in_dim(offset_rows, 2 * group_id, 2, 0)
    query_split = query_cols.reshape(block_rows, 2, head_dim)
    bias_block = spread_offsets(offset_group, 0, block_rows, row_count)
    scores = masked_scores(query_split, key_split, bias_block, segment, 0)
    highest = jnp.max(scores, axis=-1, keepdims=True)
    raised = jnp.exp(scores - highest)
    summed = jnp.sum(raised, axis=-1, keepdims=True)
    weights_low = (raised / summed).astype(jnp.bfloat16)
    context = jnp.einsum(
        "hqk,khd->qhd", weights_low, value_split, preferred_element_type=jnp.float32
    )
    context_parts = [context.reshape(block_rows, lane_count).astype(jnp.bfloat16)]
    total_parts = [(highest + jnp.log(summed))[:, :, 0]]
    return (jnp.concatenate(context_parts, axis=0), jnp.concatenate(total_parts, axis=1))


def attend_backward(
    projected, offset_rows, segment, context_grad, log_totals, group_id, head_dim, block_rows
):
    row_count = projected.shape[0]
    lane_count = 2 * head_dim
    query_cols, key_cols, value_cols = group_slices(projected, group_id, head_dim)
    key_split = key_cols.reshape(row_count, 2, head_dim)
    value_split = value_cols.reshape(row_count, 2, head_dim)
    offset_group = lax.dynamic_slice_in_dim(offset_rows, 2 * group_id, 2, 0)
    grad_cols = lax.dynamic_slice_in_dim(context_grad, group_id * lane_count, lane_count, 1)
    group_totals = lax.dynamic_slice_in_dim(log_totals, 2 * group_id, 2, 0)
    key_grad = jnp.zeros((row_count, 2, head_dim), jnp.float32)
    value_grad = jnp.zeros((row_count, 2, head_dim), jnp.float32)
    query_split = query_cols.reshape(block_rows, 2, head_dim)
    bias_block, bias_pull = jax.vjp(
        partial(spread_offsets, first_row=0, block_rows=block_rows, key_count=row_count),
        offset_group,
    )
    scores = masked_scores(query_split, key_split, bias_block, segment, 0)
    weights_full = jnp.exp(scores - group_totals[:, 0:block_rows, None])
    grad_split = grad_cols.reshape(block_rows, 2, head_dim)
    value_grad = value_grad + jnp.einsum(
        "hqk,qhd->khd",
        weights_full.astype(jnp.bfloat16),
        grad_split,
        preferred_element_type=jnp.float32,
    )
    weight_grad = jnp.einsum(
        "qhd,khd->hqk", grad_split, value_split, preferred_element_type=jnp.float32
    )
    centred = jnp.sum(weights_full * weight_grad, axis=-1, keepdims=True)
    score_grad = (weights_full * (weight_grad - centred)).astype(jnp.bfloat16)
    query_grad = jnp.einsum(
        "hqk,khd->qhd", score_grad, key_split, preferred_element_type=jnp.float32
    )
    query_parts = [query_grad.reshape(block_rows, lane_count).astype(jnp.bfloat16)]
    key_grad = key_grad + jnp.einsum(
        "hqk,qhd->khd", score_grad, query_split, preferred_element_type=jnp.float32
    )
    offset_grad = bias_pull(score_grad.astype(jnp.float32))[0]
    return (
        jnp.concatenate(query_parts, axis=0),
        key_grad.reshape(row_count, lane_count).astype(jnp.bfloat16),
        value_grad.reshape(row_count, lane_count).astype(jnp.bfloat16),
        offset_grad,
    )


def per_device(
    tokens,
    attn_gain,
    qkv_weight,
    out_weight,
    ffn_gain,
    router_weight,
    inner_weight,
    outer_weight,
    bias_table,
    lengths,
    routes,
    buckets,
    out_cotangent,
):
    row_count, model_width = tokens.shape
    head_count = bias_table.shape[1]
    bucket_count = bias_table.shape[0]
    head_dim = model_width // head_count
    groups = head_count // 2
    experts = inner_weight.shape[0]
    block_rows = min(512, row_count)
    capacity = CAP
    gains_first, qkv_full, out_full, gains_second, router_full = (
        lax.all_gather(attn_gain, ("dp", "fsdp"), axis=0, tiled=True),
        lax.all_gather(qkv_weight, ("dp", "fsdp"), axis=0, tiled=True),
        lax.all_gather(out_weight, ("dp", "fsdp"), axis=0, tiled=True),
        lax.all_gather(ffn_gain, ("dp", "fsdp"), axis=0, tiled=True),
        lax.all_gather(router_weight, ("dp", "fsdp"), axis=0, tiled=True),
    )
    inner_full, outer_full = (
        lax.all_gather(inner_weight, ("dp", "fsdp"), axis=1, tiled=True),
        lax.all_gather(outer_weight, ("dp", "fsdp"), axis=1, tiled=True),
    )
    hidden_width = outer_full.shape[1]
    position = jnp.arange(row_count, dtype=jnp.int32)
    seq_ends = jnp.cumsum(lengths[0])
    segment = jnp.sum((position[:, None] >= seq_ends[None, :]).astype(jnp.int32), axis=1)
    live_rows = (position < seq_ends[-1]).astype(jnp.float32)[:, None]
    one_hot = (buckets[:, None] == jnp.arange(bucket_count, dtype=jnp.int32)[None, :]).astype(
        jnp.float32
    )
    offset_rows = lax.dot_general(
        bias_table,
        one_hot,
        (((0,), (1,)), ((), ())),
        precision=HIGHEST,
        preferred_element_type=jnp.float32,
    )
    inputs = tokens.astype(jnp.float32)
    first_gain = gains_first.astype(jnp.float32)
    normed = rms_scale(inputs, first_gain).astype(jnp.bfloat16)
    projected = jnp.dot(normed, qkv_full, preferred_element_type=jnp.float32).astype(jnp.bfloat16)

    def forward_group(group_id):
        return attend_forward(projected, offset_rows, segment, group_id, head_dim, block_rows)

    context_groups, total_groups = lax.map(forward_group, jnp.arange(groups, dtype=jnp.int32))
    context = jnp.transpose(context_groups, (1, 0, 2)).reshape(row_count, model_width)
    log_totals = total_groups.reshape(head_count, row_count)
    attended = jnp.dot(context, out_full, preferred_element_type=jnp.float32)
    middle = inputs + live_rows * attended
    second_gain = gains_second.astype(jnp.float32)
    normed_two = rms_scale(middle, second_gain).astype(jnp.bfloat16)
    logits = jnp.dot(normed_two, router_full, preferred_element_type=jnp.float32)
    logit_top = jnp.max(logits, axis=1, keepdims=True)
    raised = jnp.exp(logits - logit_top)
    router_probs = raised / jnp.sum(raised, axis=1, keepdims=True)
    route_col = routes[:, 0]
    chosen = route_col[:, None] == jnp.arange(experts, dtype=jnp.int32)[None, :]
    chosen_weight = chosen.astype(jnp.float32)
    gating = jnp.sum(router_probs * chosen_weight, axis=1, keepdims=True)
    rank_in = jnp.cumsum(chosen.astype(jnp.int32), axis=0) - 1
    slot_of = jnp.sum(jnp.where(chosen, rank_in, 0), axis=1)
    filled = jnp.sum(chosen.astype(jnp.int32), axis=0)
    dispatch = jnp.zeros((experts, capacity), jnp.int32).at[route_col, slot_of].set(position)
    valid_slots = (jnp.arange(capacity, dtype=jnp.int32)[None, :] < filled[:, None])[:, :, None]
    expert_rows = normed_two[dispatch]
    gate_up = jnp.einsum(
        "ecd,edf->ecf", expert_rows, inner_full, preferred_element_type=jnp.float32
    )
    activated = gated_unit(gate_up).astype(jnp.bfloat16)
    expert_out = jnp.einsum(
        "ecf,efd->ecd", activated, outer_full, preferred_element_type=jnp.float32
    )
    combined = expert_out[route_col, slot_of]
    mixed = (middle + live_rows * gating * combined).astype(jnp.bfloat16)
    gains_first, qkv_full, out_full, gains_second, router_full = (
        lax.all_gather(attn_gain, ("dp", "fsdp"), axis=0, tiled=True),
        lax.all_gather(qkv_weight, ("dp", "fsdp"), axis=0, tiled=True),
        lax.all_gather(out_weight, ("dp", "fsdp"), axis=0, tiled=True),
        lax.all_gather(ffn_gain, ("dp", "fsdp"), axis=0, tiled=True),
        lax.all_gather(router_weight, ("dp", "fsdp"), axis=0, tiled=True),
    )
    inner_full, outer_full = (
        lax.all_gather(inner_weight, ("dp", "fsdp"), axis=1, tiled=True),
        lax.all_gather(outer_weight, ("dp", "fsdp"), axis=1, tiled=True),
    )
    first_back = gains_first.astype(jnp.float32)
    second_back = gains_second.astype(jnp.float32)
    cotangent = out_cotangent.astype(jnp.float32)
    branch_grad = live_rows * cotangent
    combined_grad = branch_grad * gating
    gating_grad = jnp.sum(branch_grad * combined, axis=1, keepdims=True)
    slot_grad = jnp.where(valid_slots, combined_grad[dispatch], 0.0).astype(jnp.bfloat16)
    outer_sum = jnp.einsum("ecf,ecd->fed", activated, slot_grad, preferred_element_type=jnp.float32)
    act_grad = jnp.einsum("ecd,efd->ecf", slot_grad, outer_full, preferred_element_type=jnp.float32)
    unit_pull = jax.vjp(gated_unit, gate_up)[1]
    gate_up_grad = unit_pull(act_grad)[0].astype(jnp.bfloat16)
    inner_sum = jnp.einsum(
        "ecd,ecf->def", expert_rows, gate_up_grad, preferred_element_type=jnp.float32
    )
    rows_grad = jnp.einsum(
        "ecf,edf->ecd", gate_up_grad, inner_full, preferred_element_type=jnp.float32
    )
    prob_grad = chosen_weight * gating_grad
    logit_grad = router_probs * (
        prob_grad - jnp.sum(router_probs * prob_grad, axis=1, keepdims=True)
    )
    router_sum = lax.dot_general(
        normed_two.astype(jnp.float32),
        logit_grad,
        (((0,), (0,)), ((), ())),
        precision=HIGHEST,
        preferred_element_type=jnp.float32,
    )
    normed_two_grad = rows_grad[route_col, slot_of] + lax.dot_general(
        logit_grad,
        router_full.astype(jnp.float32),
        (((1,), (1,)), ((), ())),
        precision=HIGHEST,
        preferred_element_type=jnp.float32,
    )
    norm_two_pull = jax.vjp(rms_scale, middle, second_back)[1]
    middle_part, second_gain_sum = norm_two_pull(normed_two_grad)
    middle_grad = cotangent + middle_part
    attended_grad = (live_rows * middle_grad).astype(jnp.bfloat16)
    out_sum = contract_rows(context, attended_grad)
    context_grad = contract_cols(attended_grad, out_full).astype(jnp.bfloat16)

    def backward_group(group_id):
        return attend_backward(
            projected,
            offset_rows,
            segment,
            context_grad,
            log_totals,
            group_id,
            head_dim,
            block_rows,
        )

    query_groups, key_groups, value_groups, offset_groups = lax.map(
        backward_group, jnp.arange(groups, dtype=jnp.int32)
    )

    def regroup(stacked):
        return jnp.transpose(stacked, (1, 0, 2)).reshape(row_count, model_width)

    projected_grad = jnp.concatenate(
        [regroup(query_groups), regroup(key_groups), regroup(value_groups)], axis=1
    )
    qkv_sum = contract_rows(normed, projected_grad)
    normed_grad = contract_cols(projected_grad, qkv_full)
    norm_one_pull = jax.vjp(rms_scale, inputs, first_back)[1]
    input_part, first_gain_sum = norm_one_pull(normed_grad)
    tokens_grad = middle_grad + input_part
    offset_grad = offset_groups.reshape(head_count, -1)
    table_part = lax.dot_general(
        one_hot,
        offset_grad,
        (((0,), (1,)), ((), ())),
        precision=HIGHEST,
        preferred_element_type=jnp.float32,
    )
    width_rows = jnp.concatenate(
        [
            first_gain_sum[:, None],
            qkv_sum,
            out_sum,
            second_gain_sum[:, None],
            router_sum,
            inner_sum.reshape(model_width, experts * 2 * hidden_width),
        ],
        axis=1,
    )
    hidden_rows = outer_sum.reshape(hidden_width, experts * model_width)
    width_share, hidden_share = (
        lax.psum_scatter(width_rows, ("dp", "fsdp"), scatter_dimension=0, tiled=True),
        lax.psum_scatter(hidden_rows, ("dp", "fsdp"), scatter_dimension=0, tiled=True),
    )
    own_rows = width_share.shape[0]
    own_hidden = hidden_share.shape[0]
    column = 0
    attn_gain_grad = width_share[:, column]
    column = column + 1
    qkv_weight_grad = width_share[:, column : column + 3 * model_width]
    column = column + 3 * model_width
    out_weight_grad = width_share[:, column : column + model_width]
    column = column + model_width
    ffn_gain_grad = width_share[:, column]
    column = column + 1
    router_grad = width_share[:, column : column + experts]
    column = column + experts
    inner_grad = jnp.transpose(
        width_share[:, column:].reshape(own_rows, experts, 2 * hidden_width), (1, 0, 2)
    )
    outer_grad = jnp.transpose(hidden_share.reshape(own_hidden, experts, model_width), (1, 0, 2))
    table_grad = lax.psum(table_part, ("dp", "fsdp"))
    return (
        mixed,
        tokens_grad,
        attn_gain_grad,
        qkv_weight_grad,
        out_weight_grad,
        ffn_gain_grad,
        router_grad,
        inner_grad,
        outer_grad,
        table_grad,
    )


def solution(mesh):
    placed = (
        P(("dp", "fsdp"), None),
        P(("dp", "fsdp")),
        P(("dp", "fsdp"), None),
        P(("dp", "fsdp"), None),
        P(("dp", "fsdp")),
        P(("dp", "fsdp"), None),
        P(None, ("dp", "fsdp"), None),
        P(None, ("dp", "fsdp"), None),
        P(),
        P(("dp", "fsdp"), None),
        P(("dp", "fsdp"), None),
        P(),
        P(("dp", "fsdp"), None),
    )
    return jax.shard_map(
        per_device,
        mesh=mesh,
        in_specs=placed,
        out_specs=(
            P(("dp", "fsdp"), None),
            P(("dp", "fsdp"), None),
            P(("dp", "fsdp")),
            P(("dp", "fsdp"), None),
            P(("dp", "fsdp"), None),
            P(("dp", "fsdp")),
            P(("dp", "fsdp"), None),
            P(None, ("dp", "fsdp"), None),
            P(None, ("dp", "fsdp"), None),
            P(),
        ),
        check_vma=False,
    )
```

profile of v0, /device:TPU:0, one launch (start us, length us, event | category | flops | bytes accessed | tf_op | source)
XLA Modules:
  0.0 1794.8 jit_solution(13498637168202635689)
XLA Ops:
  16.9 24.5 %scatter_fusion = s32[2,320]{1,0:T(2,128)S(1)} fusion(s32[2,320]{1,0:T(2,128)S(1)} %broadcast.242, s32[512]{0:T(512)S(1)} %bitcast.205, s32[512]{0:T(512)S(1)} %iota.39), kind=kCustom, calls=%fused_computation.4 | custom fusion | bytes 10240 | tf_op jit(solution)/shard_map/scatter | solution.py:216
  43.8 42.2 %all-reduce.9 = (bf16[768]{0:T(1024)(128)(2,1)S(1)}, bf16[768]{0:T(1024)(128)(2,1)S(1)}) all-reduce(bf16[768]{0:T(1024)(128)(2,1)S(1)} %dynamic-update-slice, bf16[768]{0:T(1024)(128)(2,1)S(1)} %dynamic-update-slice.1), channel_id=1, replica_groups=mesh['dp'=8,'fsdp'=4] {'dp','fsdp'}, use_global_device_ids=true, to_apply=%add.6 | all-reduce | flops 1536 | bytes 6144
  86.5 40.1 %all-gather = bf16[32,24,2]{1,2,0:T(2,128)(2,1)S(1)} all-gather(bf16[1,24,2]{1,2,0:T(2,128)(2,1)S(1)} %bitcast.240), channel_id=1, replica_groups=mesh['dp'=8,'fsdp'=4] {'dp','fsdp'}, dimensions={0}, use_global_device_ids=true | all-gather | bytes 3168 | tf_op jit(solution)/shard_map/all_gather | solution.py:169
  128.4 5.6 convolution_convert_fusion.4
  140.0 188.3 %while.32 = (s32[]{:T(128)}, bf16[6,512,128]{1,2,0:T(8,128)(2,1)}, f32[6,2,512]{2,1,0:T(2,128)}, s32[6]{0:T(128)}, bf16[512,2304]{0,1:T(8,128)(2,1)}, /*index=5*...) while((s32[]{:T(128)}, bf16[6,512,128]{1,2,0:T(8,128)(2,1)}, ...), condition=%wide.region_6.7_spmd, body=%wide.region_3.6_spmd.sunk | while | flops 138738704 | bytes 50391436 | solution.py:198
  148.4 5.6 slice.106
  154.0 9.4 reshape.471
  179.5 5.6 slice.106
  185.1 9.4 reshape.471
  211.4 5.6 slice.106
  217.0 9.6 reshape.471
  242.6 5.6 slice.106
  248.3 9.5 reshape.471
  273.8 5.6 slice.106
  279.5 9.4 reshape.471
  305.0 5.6 slice.106
  310.6 9.5 reshape.471
  336.7 10.8 fusion.58
  347.5 5.5 copy-done.2
  357.0 8.1 fusion.59
  365.1 7.4 gather_fusion.1
  377.8 18.8 %fusion.9 = (f32[2,320,3072]{2,1,0:T(8,128)}, f32[2,320,3072]{2,1,0:T(8,128)}) fusion(f32[2,320,6144]{2,1,0:T(8,128)} %copy-done.2, bf16[2,3072,768]{2,1,0:T(8,128)(2,1)} %all-gather.12.cloned.1.call-done, bf16[2,320,768]{2,1,0:T(8,128)(2,1)S(1)} %bitcast.221, pred[2,320]{1,0:T(4,128)(4,1)S(1)} %copy-done.27), kind=kOutput, calls=%fused_computation.57 | convolution fusion | flops 3063644160 | bytes 41878144 | tf_op jit(solution)/shard_map/ecd,efd->ecf/dot_general | solution.py:247
  396.6 25.1 %fusion.20 = f32[2,6144,768]{2,1,0:T(8,128)} fusion(bf16[2,320,768]{2,1,0:T(8,128)(2,1)S(1)} %bitcast.214, f32[2,320,3072]{2,1,0:T(8,128)} %get-tuple-element.424, f32[2,320,3072]{2,1,0:T(8,128)} %get-tuple-element.423), kind=kOutput, calls=%fused_computation.82 | convolution fusion | flops 6047662080 | bytes 54460416 | tf_op jit(solution)/shard_map/ecd,ecf->def/dot_general | solution.py:250
  421.7 19.6 %fusion.21 = f32[2,320,768]{2,1,0:T(8,128)S(1)} fusion(bf16[2,768,6144]{2,1,0:T(8,128)(2,1)} %all-gather.10.cloned.1.call-done, f32[2,320,3072]{2,1,0:T(8,128)} %get-tuple-element.424, f32[2,320,3072]{2,1,0:T(8,128)} %get-tuple-element.423), kind=kOutput, calls=%fused_computation.83 | convolution fusion | flops 6047662080 | bytes 36569088 | tf_op jit(solution)/shard_map/ecf,edf->ecd/dot_general | solution.py:253
  441.3 7.4 gather_fusion.3
  462.4 301.7 %while.33 = (s32[]{:T(128)}, bf16[6,512,128]{1,2,0:T(8,128)(2,1)}, bf16[6,512,128]{1,2,0:T(8,128)(2,1)}, bf16[6,512,128]{1,2,0:T(8,128)(2,1)}, f32[6,2,1023]{2,1...) while((s32[]{:T(128)}, bf16[6,512,128]{1,2,0:T(8,128)(2,1)}, ...), condition=%wide.region_22.23_spmd, body=%wide.region_19.22_spmd.sunk | while | flops 342815744 | bytes 90696264 | solution.py:293
  472.0 5.6 slice.108
  477.6 9.4 reshape.473
  522.2 5.6 slice.108
  527.8 9.4 reshape.473
  572.4 5.6 slice.108
  578.0 9.4 reshape.473
  622.5 5.6 slice.108
  628.1 9.4 reshape.473
  672.8 5.6 slice.108
  678.3 9.4 reshape.473
  722.9 5.6 slice.108
  728.5 9.4 reshape.473
  764.3 7.0 fusion.22
  771.4 4.7 fusion.15
  776.1 114.2 %concatenate.19 = f32[768,15364]{0,1:T(8,128)} concatenate(f32[768,1]{0,1:T(1,128)S(1)} %broadcast_in_dim.132, f32[768,2304]{0,1:T(8,128)} %fusion.22, f32[768,768]{0,1:T(8,128)S(1)} %copy-done.10, f32[768,1]{0,1:T(1,128)S(1)} %copy-done.37, f32[768,2]{0,1:T(2,128)S(1)} %copy-done.32, f32[768,12288]{0,1:T(8,128)} %bitcast.201), dimensions={1} | concatenate | bytes 94396416 | tf_op jit(solution)/shard_map/concatenate | solution.py:316
  891.5 12.2 fusion.25
  903.7 18.8 %copy.82 = f32[3072,1536]{1,0:T(8,128)} copy(f32[3072,1536]{0,1:T(8,128)} %bitcast.204) | data formatting | bytes 37748736 | tf_op jit(solution)/shard_map/reshape | solution.py:327
  923.7 38.4 %psum.7 = f32[32,12]{0,1:T(8,128)} all-reduce(f32[32,12]{0,1:T(8,128)S(1)} %fusion.24), channel_id=1, replica_groups=mesh['dp'=8,'fsdp'=4] {'dp','fsdp'}, use_global_device_ids=true, to_apply=%region_28.29 | all-reduce | flops 384 | bytes 3072 | tf_op jit(solution)/shard_map/psum | solution.py:349
  965.2 607.2 %all-reduce.12.cloned.1.call-done = f32[768,15364]{0,1:T(8,128)} async-done(((f32[768,15364]{0,1:T(8,128)}), f32[768,15364]{0,1:T(8,128)}) %all-reduce.12.cloned.1.call-update) | async-done | bytes 47198224
  1577.5 7.2 dynamic-slice.6
  1584.7 4.7 copy.92
  1593.7 191.7 %reduce-scatter.3.cloned.1.call-done = f32[96,1536]{1,0:T(8,128)} async-done(((f32[3072,1536]{1,0:T(8,128)}), f32[96,1536]{1,0:T(8,128)}) %reduce-scatter.3.cloned.1.call-update) | async-done | bytes 589840 | tf_op jit(solution)/shard_map/reduce_scatter | solution.py:330
  (481 shorter events, 360.3 us)
Async XLA Ops:
  7.2 120.2 %copy-start = (f32[32,12]{0,1:T(8,128)S(1)}, f32[32,12]{0,1:T(8,128)}, u32[]{:S(2)}) copy-start(f32[32,12]{0,1:T(8,128)} %param.25) | copy-start | bytes 4612
  7.2 121.2 %all-gather.6.cloned.1.call-start = ((), (), s32[]{:S(2)}) async-start(), calls=%async_computation.1 | async-start | bytes 3649536 | tf_op jit(solution)/shard_map/all_gather | solution.py:166
  7.9 321.1 %all-gather.8.cloned.1.call-start = ((), (), s32[]{:S(2)}) async-start(), calls=%async_computation.2 | async-start | bytes 1216512 | tf_op jit(solution)/shard_map/all_gather | solution.py:167
  8.7 328.0 %all-gather.10.cloned.1.call-start = ((), (), s32[]{:S(2)}) async-start(), calls=%async_computation.3 | async-start | bytes 19464192 | tf_op jit(solution)/shard_map/all_gather | solution.py:172
  9.4 347.5 %all-gather.12.cloned.1.call-start = ((), (), s32[]{:S(2)}) async-start(), calls=%async_computation.4 | async-start | bytes 9732096 | tf_op jit(solution)/shard_map/all_gather | solution.py:173
  10.0 1562.4 %all-reduce.12.cloned.1.call-start = ((), (), s32[]{:S(2)}) async-start(), calls=%async_computation.6 | async-start | bytes 94420992
  12.9 114.4 %copy-start.33 = (f32[512]{0:T(512)}, f32[512]{0:T(512)S(1)}, u32[]{:S(2)}) copy-start(f32[512]{0:T(512)S(1)} %fusion.18) | copy-start | bytes 6148
  16.8 26.5 %copy-start.45 = (bf16[24]{0:T(256)(128)(2,1)S(1)}, bf16[24]{0:T(256)(128)(2,1)}, u32[]{:S(2)}) copy-start(bf16[24]{0:T(256)(128)(2,1)} %param.18) | copy-start | bytes 148
  16.8 26.7 %copy-start.46 = (bf16[24]{0:T(256)(128)(2,1)S(1)}, bf16[24]{0:T(256)(128)(2,1)}, u32[]{:S(2)}) copy-start(bf16[24]{0:T(256)(128)(2,1)} %param.21) | copy-start | bytes 148
  16.8 69.7 %copy-start.40 = (bf16[24,2]{0,1:T(2,128)(2,1)S(1)}, bf16[24,2]{0,1:T(2,128)(2,1)}, u32[]{:S(2)}) copy-start(bf16[24,2]{0,1:T(2,128)(2,1)} %param.22) | copy-start | bytes 292
  16.8 110.5 %copy-start.43 = (s32[1023]{0:T(1024)S(1)}, s32[1023]{0:T(1024)}, u32[]{:S(2)}) copy-start(s32[1023]{0:T(1024)} %param.28) | copy-start | bytes 12280
  16.9 111.6 %copy-start.15 = (bf16[512,768]{1,0:T(8,128)(2,1)S(1)}, bf16[512,768]{1,0:T(8,128)(2,1)}, u32[]{:S(2)}) copy-start(bf16[512,768]{1,0:T(8,128)(2,1)} %param.17) | copy-start | bytes 2359300
  85.9 48.1 %copy-start.35 = (f32[768]{0:T(1024)}, f32[768]{0:T(1024)S(1)}, u32[]{:S(2)}) copy-start(f32[768]{0:T(1024)S(1)} %convert_element_type.164) | copy-start | bytes 9220
  127.3 6.7 copy-start.38
  329.0 3.6 copy-start.25
  332.9 3.4 copy-start.30
  347.4 5.5 copy-start.2
  365.0 7.4 copy-start.29
  377.8 18.8 %copy-start.13 = (bf16[640,768]{1,0:T(8,128)(2,1)}, bf16[640,768]{1,0:T(8,128)(2,1)S(1)}, u32[]{:S(2)}) copy-start(bf16[640,768]{1,0:T(8,128)(2,1)S(1)} %gather_fusion.2) | copy-start | bytes 2949124
  377.8 18.8 %copy-start.3 = (bf16[640,768]{1,0:T(8,128)(2,1)S(1)}, bf16[640,768]{1,0:T(8,128)(2,1)}, u32[]{:S(2)}) copy-start(bf16[640,768]{1,0:T(8,128)(2,1)} %gather_fusion) | copy-start | bytes 2949124
  449.7 4.5 copy-start.4
  449.7 4.5 copy-start.8
  449.7 4.5 copy-start.12
  462.8 4.9 copy-start.20
  462.8 4.9 copy-start.22
  513.1 4.8 copy-start.20
  513.1 4.8 copy-start.22
  563.3 4.8 copy-start.20
  563.3 4.8 copy-start.22
  613.4 4.8 copy-start.20
  613.4 4.8 copy-start.22
  663.7 4.8 copy-start.20
  663.7 4.8 copy-start.22
  713.8 4.8 copy-start.20
  713.8 4.8 copy-start.22
  764.2 7.1 copy-start.16
  764.2 7.1 copy-start.18
  764.2 7.1 copy-start.19
  764.2 7.1 copy-start.36
  764.2 7.1 copy-start.39
  764.3 7.1 copy-start.41
  771.3 4.7 copy-start.10
  771.3 4.7 copy-start.32
  771.4 4.7 copy-start.37
  890.3 895.1 %reduce-scatter.3.cloned.1.call-start = ((), (), s32[]{:S(2)}) async-start(), calls=%async_computation.5 | async-start | bytes 19464192 | tf_op jit(solution)/shard_map/reduce_scatter | solution.py:330
  922.5 39.7 %copy-start.34 = (f32[512]{0:T(512)S(1)}, f32[512]{0:T(512)}, u32[]{:S(2)}) copy-start(f32[512]{0:T(512)} %copy-done.33) | copy-start | bytes 6148
  922.5 39.7 %copy-start.6 = (f32[512,768]{1,0:T(8,128)S(1)}, f32[512,768]{1,0:T(8,128)}, u32[]{:S(2)}) copy-start(f32[512,768]{1,0:T(8,128)} %copy-done.5) | copy-start | bytes 4718596
  1589.4 198.4 %copy-start.1 = (f32[32,12]{0,1:T(8,128)S(1)}, f32[32,12]{0,1:T(8,128)}, u32[]{:S(2)}) copy-start(f32[32,12]{0,1:T(8,128)} %param.25) | copy-start | bytes 4612
  (36 other events, 63.4 us)
Sparse Core Ops, SparseCore 0:
  10.9 63.1 all-gather.5
  77.0 52.7 all-gather.7
  132.7 123.6 all-gather.9
  259.0 80.3 all-gather.11
  890.4 681.9 all-reduce.11
  1579.8 205.6 reduce-scatter.2
where the time goes:
time: 1810 us; the launch traced here: 1790 us
  waiting for transfers between devices  802 us (44%)
  local copies, waits for them, and re-layouts  616 us (34%)
  matrix products  170 us (9%)
  blocking collectives  121 us (7%)
  other arithmetic  54.2 us (3%)
    unnamed x7, waiting for transfers between devices  610 us
    reduce_scatter x1, waiting for transfers between devices, per_device(): lax.psum_scatter(hidden_rows, ('dp', 'fsdp'), scatter_dimension=0, tiled=...  192 us
    reshape x18, local copies, waits for them, and re-layouts, spread_offsets(): return shifted.reshape(lane_count, block_rows, window)[:, :, :key_count]  126 us
    concatenate x1, local copies, waits for them, and re-layouts, per_device(): jnp.concatenate([first_gain_sum[:, None], qkv_sum, out_sum, second_gain_s...  114 us
    while x108, local copies, waits for them, and re-layouts  107 us
    slice x12, local copies, waits for them, and re-layouts, spread_offsets(): shifted = repeated[:, block_rows - 1:block_rows - 1 + block_rows * window]  67.2 us
    unnamed x1, blocking collectives  42.2 us
    all_gather x1, blocking collectives, per_device(): lax.all_gather(router_weight, ('dp', 'fsdp'), axis=0, tiled=True)  40.1 us
  transfers between devices with their start and end apart: 6, of which 2 were waited for; matrix products, arithmetic and copies ran while one was open for 16% of the time, Pallas kernels for 0%

commit v1 on v0

v1 whole, which is shorter than its diff:
```python
import jax
import jax.numpy as jnp
from jax import lax
from jax.experimental import pallas as pl
from jax.experimental.pallas import tpu as pltpu
from jax.sharding import PartitionSpec as P

CAP = 320
HEAD_DIM = 64


EPSILON = 1e-06
NEGATIVE = -1e30
HIGHEST = lax.Precision.HIGHEST


def rms_scale(values, gain_row):
    return (
        values * lax.rsqrt(jnp.mean(values * values, axis=-1, keepdims=True) + EPSILON) * gain_row
    )


def gated_unit(gate_up):
    hidden_units = gate_up.shape[-1] // 2
    return jax.nn.gelu(gate_up[..., :hidden_units], approximate=True) * gate_up[..., hidden_units:]


def contract_rows(left_side, right_side):
    return lax.dot_general(
        left_side, right_side, (((0,), (0,)), ((), ())), preferred_element_type=jnp.float32
    )


def contract_cols(left_side, right_side):
    return lax.dot_general(
        left_side, right_side, (((1,), (1,)), ((), ())), preferred_element_type=jnp.float32
    )


def head_lanes(values, head):
    lane = lax.broadcasted_iota(jnp.int32, values.shape, 1)
    return jnp.where((lane // HEAD_DIM) == head, values, jnp.zeros_like(values))


def forward_kernel(query_ref, key_ref, value_ref, offset_ref, seg_col_ref, seg_row_ref, context_ref, weight_ref):
    rows = query_ref.shape[0]
    same_doc = seg_col_ref[...] == seg_row_ref[...]
    query, key, value = query_ref[...], key_ref[...], value_ref[...]
    context = None
    for head in range(2):
        wide = jnp.broadcast_to(offset_ref[0, head : head + 1, :], (rows, 2 * rows))
        bias = pltpu.roll(wide, rows + 1, 1, stride=1, stride_axis=0)[:, :rows]
        scores = contract_cols(head_lanes(query, head), key) + bias
        scores = jnp.where(same_doc, scores, NEGATIVE)
        highest = jnp.max(scores, axis=-1, keepdims=True)
        raised = jnp.exp(scores - highest)
        weights = raised / jnp.sum(raised, axis=-1, keepdims=True)
        weight_ref[head] = weights
        part = jnp.dot(weights.astype(jnp.bfloat16), value, preferred_element_type=jnp.float32)
        part = head_lanes(part, head)
        context = part if context is None else context + part
    context_ref[...] = context.astype(jnp.bfloat16)


def attend_forward(projected, offset_pad, segment):
    rows, width = projected.shape
    groups = width // 3 // 128
    col = lambda part: pl.BlockSpec((rows, 128), lambda g: (0, part * groups + g))
    return pl.pallas_call(
        forward_kernel,
        grid=(groups,),
        in_specs=[
            col(0),
            col(1),
            col(2),
            pl.BlockSpec((1, 2, 2 * rows), lambda g: (g, 0, 0)),
            pl.BlockSpec((rows, 1), lambda g: (0, 0)),
            pl.BlockSpec((1, rows), lambda g: (0, 0)),
        ],
        out_specs=[
            pl.BlockSpec((rows, 128), lambda g: (0, g)),
            pl.BlockSpec((2, rows, rows), lambda g: (g, 0, 0)),
        ],
        out_shape=[
            jax.ShapeDtypeStruct((rows, width // 3), jnp.bfloat16),
            jax.ShapeDtypeStruct((2 * groups, rows, rows), jnp.float32),
        ],
        compiler_params=pltpu.CompilerParams(vmem_limit_bytes=48 * 1024 * 1024),
        cost_estimate=pl.CostEstimate(
            flops=8 * groups * rows * rows * 128, bytes_accessed=2**24, transcendentals=2**22
        ),
    )(
        projected,
        projected,
        projected,
        offset_pad.reshape(groups, 2, 2 * rows),
        segment[:, None],
        segment[None, :],
    )


def backward_kernel(
    query_ref, key_ref, value_ref, grad_ref, weight_ref, dq_ref, dk_ref, dv_ref, offset_ref
):
    rows = query_ref.shape[0]
    query, key, value, grad = query_ref[...], key_ref[...], value_ref[...], grad_ref[...]
    row_id = lax.broadcasted_iota(jnp.int32, (rows, rows), 0)
    col_id = lax.broadcasted_iota(jnp.int32, (rows, rows), 1)
    flip = jnp.where(row_id + col_id == rows - 1, 1.0, 0.0).astype(jnp.bfloat16)
    dq = dk = dv = None
    for head in range(2):
        weights = weight_ref[head]
        weight_grad = contract_cols(head_lanes(grad, head), value)
        product = weights * weight_grad
        centred = jnp.sum(product, axis=-1, keepdims=True)
        score_grad = (product - weights * centred).astype(jnp.bfloat16)
        part_v = head_lanes(contract_rows(weights.astype(jnp.bfloat16), grad), head)
        part_k = head_lanes(contract_rows(score_grad, query), head)
        part_q = head_lanes(
            jnp.dot(score_grad, key, preferred_element_type=jnp.float32), head
        )
        dv = part_v if dv is None else dv + part_v
        dk = part_k if dk is None else dk + part_k
        dq = part_q if dq is None else dq + part_q
        turned = jnp.dot(flip, score_grad, preferred_element_type=jnp.float32)
        wide = jnp.concatenate([turned, jnp.zeros((rows, rows), jnp.float32)], axis=1)
        skewed = pltpu.roll(wide, 0, 1, stride=1, stride_axis=0)
        offset_ref[0, head : head + 1, :] = jnp.sum(skewed, axis=0, keepdims=True)
    dq_ref[...] = dq.astype(jnp.bfloat16)
    dk_ref[...] = dk.astype(jnp.bfloat16)
    dv_ref[...] = dv.astype(jnp.bfloat16)


def attend_backward(projected, context_grad, weights):
    rows, width = projected.shape
    groups = width // 3 // 128
    col = lambda part: pl.BlockSpec((rows, 128), lambda g: (0, part * groups + g))
    grad_shape = jax.ShapeDtypeStruct((rows, width // 3), jnp.bfloat16)
    return pl.pallas_call(
        backward_kernel,
        grid=(groups,),
        in_specs=[
            col(0),
            col(1),
            col(2),
            col(0),
            pl.BlockSpec((2, rows, rows), lambda g: (g, 0, 0)),
        ],
        out_specs=[col(0), col(0), col(0), pl.BlockSpec((1, 2, 2 * rows), lambda g: (g, 0, 0))],
        out_shape=[grad_shape] * 3 + [jax.ShapeDtypeStruct((groups, 2, 2 * rows), jnp.float32)],
        compiler_params=pltpu.CompilerParams(vmem_limit_bytes=48 * 1024 * 1024),
        cost_estimate=pl.CostEstimate(
            flops=24 * groups * rows * rows * 128, bytes_accessed=2**24, transcendentals=0
        ),
    )(projected, projected, projected, context_grad, weights)


def per_device(
    tokens,
    attn_gain,
    qkv_weight,
    out_weight,
    ffn_gain,
    router_weight,
    inner_weight,
    outer_weight,
    bias_table,
    lengths,
    routes,
    buckets,
    out_cotangent,
):
    row_count, model_width = tokens.shape
    head_count = bias_table.shape[1]
    bucket_count = bias_table.shape[0]
    head_dim = model_width // head_count
    experts = inner_weight.shape[0]
    capacity = CAP
    both = ("dp", "fsdp")
    packed = jnp.concatenate(
        [
            qkv_weight,
            out_weight,
            attn_gain[:, None],
            ffn_gain[:, None],
            router_weight,
            jnp.zeros((attn_gain.shape[0], 128 - 2 - experts), jnp.bfloat16),
        ],
        axis=1,
    )
    packed_full = lax.all_gather(packed, both, axis=0, tiled=True)
    qkv_full = packed_full[:, : 3 * model_width]
    out_full = packed_full[:, 3 * model_width : 4 * model_width]
    gains_first = packed_full[:, 4 * model_width]
    gains_second = packed_full[:, 4 * model_width + 1]
    router_full = packed_full[:, 4 * model_width + 2 : 4 * model_width + 2 + experts]
    inner_full = lax.all_gather(inner_weight, both, axis=1, tiled=True)
    outer_full = lax.all_gather(outer_weight, both, axis=1, tiled=True)
    hidden_width = outer_full.shape[1]
    position = jnp.arange(row_count, dtype=jnp.int32)
    seq_ends = jnp.cumsum(lengths[0])
    segment = jnp.sum((position[:, None] >= seq_ends[None, :]).astype(jnp.int32), axis=1)
    live_rows = (position < seq_ends[-1]).astype(jnp.float32)[:, None]
    one_hot = (buckets[:, None] == jnp.arange(bucket_count, dtype=jnp.int32)[None, :]).astype(
        jnp.float32
    )
    offset_rows = lax.dot_general(
        bias_table,
        one_hot,
        (((0,), (1,)), ((), ())),
        precision=HIGHEST,
        preferred_element_type=jnp.float32,
    )
    inputs = tokens.astype(jnp.float32)
    first_gain = gains_first.astype(jnp.float32)
    normed = rms_scale(inputs, first_gain).astype(jnp.bfloat16)
    projected = jnp.dot(normed, qkv_full, preferred_element_type=jnp.float32).astype(jnp.bfloat16)

    offset_pad = jnp.pad(offset_rows, ((0, 0), (0, 1)))
    context, weights = attend_forward(projected, offset_pad, segment)
    attended = jnp.dot(context, out_full, preferred_element_type=jnp.float32)
    middle = inputs + live_rows * attended
    second_gain = gains_second.astype(jnp.float32)
    normed_two = rms_scale(middle, second_gain).astype(jnp.bfloat16)
    logits = jnp.dot(normed_two, router_full, preferred_element_type=jnp.float32)
    logit_top = jnp.max(logits, axis=1, keepdims=True)
    raised = jnp.exp(logits - logit_top)
    router_probs = raised / jnp.sum(raised, axis=1, keepdims=True)
    route_col = routes[:, 0]
    chosen = route_col[:, None] == jnp.arange(experts, dtype=jnp.int32)[None, :]
    chosen_weight = chosen.astype(jnp.float32)
    gating = jnp.sum(router_probs * chosen_weight, axis=1, keepdims=True)
    rank_in = jnp.cumsum(chosen.astype(jnp.int32), axis=0) - 1
    slot_of = jnp.sum(jnp.where(chosen, rank_in, 0), axis=1)
    slot_index = route_col * capacity + slot_of
    dispatch = (
        jnp.arange(experts * capacity, dtype=jnp.int32)[:, None] == slot_index[None, :]
    ).astype(jnp.bfloat16)

    def to_slots(rows):
        return jnp.dot(dispatch, rows, preferred_element_type=jnp.float32).astype(
            jnp.bfloat16
        ).reshape(experts, capacity, -1)

    def from_slots(rows):
        rows = rows.reshape(experts * capacity, -1)
        high = lax.reduce_precision(rows, 8, 7)
        low = (rows - high).astype(jnp.bfloat16)
        return contract_rows(dispatch, high.astype(jnp.bfloat16)) + contract_rows(dispatch, low)

    expert_rows = to_slots(normed_two)
    gate_up = jnp.einsum(
        "ecd,edf->ecf", expert_rows, inner_full, preferred_element_type=jnp.float32
    )
    activated = gated_unit(gate_up).astype(jnp.bfloat16)
    expert_out = jnp.einsum(
        "ecf,efd->ecd", activated, outer_full, preferred_element_type=jnp.float32
    )
    combined = from_slots(expert_out)
    mixed = (middle + live_rows * gating * combined).astype(jnp.bfloat16)
    first_back = gains_first.astype(jnp.float32)
    second_back = gains_second.astype(jnp.float32)
    cotangent = out_cotangent.astype(jnp.float32)
    branch_grad = live_rows * cotangent
    combined_grad = branch_grad * gating
    gating_grad = jnp.sum(branch_grad * combined, axis=1, keepdims=True)
    slot_grad = to_slots(combined_grad.astype(jnp.bfloat16))
    outer_sum = jnp.einsum("ecf,ecd->efd", activated, slot_grad, preferred_element_type=jnp.float32)
    act_grad = jnp.einsum("ecd,efd->ecf", slot_grad, outer_full, preferred_element_type=jnp.float32)
    unit_pull = jax.vjp(gated_unit, gate_up)[1]
    gate_up_grad = unit_pull(act_grad)[0].astype(jnp.bfloat16)
    inner_sum = [
        contract_rows(expert_rows[expert], gate_up_grad[expert]) for expert in range(experts)
    ]
    rows_grad = jnp.einsum(
        "ecf,edf->ecd", gate_up_grad, inner_full, preferred_element_type=jnp.float32
    )
    prob_grad = chosen_weight * gating_grad
    logit_grad = router_probs * (
        prob_grad - jnp.sum(router_probs * prob_grad, axis=1, keepdims=True)
    )
    router_sum = lax.dot_general(
        normed_two.astype(jnp.float32),
        logit_grad,
        (((0,), (0,)), ((), ())),
        precision=HIGHEST,
        preferred_element_type=jnp.float32,
    )
    normed_two_grad = from_slots(rows_grad) + lax.dot_general(
        logit_grad,
        router_full.astype(jnp.float32),
        (((1,), (1,)), ((), ())),
        precision=HIGHEST,
        preferred_element_type=jnp.float32,
    )
    norm_two_pull = jax.vjp(rms_scale, middle, second_back)[1]
    middle_part, second_gain_sum = norm_two_pull(normed_two_grad)
    middle_grad = cotangent + middle_part
    attended_grad = (live_rows * middle_grad).astype(jnp.bfloat16)
    out_sum = contract_rows(context, attended_grad)
    context_grad = contract_cols(attended_grad, out_full).astype(jnp.bfloat16)

    query_grad, key_grad, value_grad, offset_groups = attend_backward(
        projected, context_grad, weights
    )
    projected_grad = jnp.concatenate([query_grad, key_grad, value_grad], axis=1)
    qkv_sum = contract_rows(normed, projected_grad)
    normed_grad = contract_cols(projected_grad, qkv_full)
    norm_one_pull = jax.vjp(rms_scale, inputs, first_back)[1]
    input_part, first_gain_sum = norm_one_pull(normed_grad)
    tokens_grad = middle_grad + input_part
    offset_grad = offset_groups.reshape(head_count, -1)[:, : buckets.shape[0]]
    table_part = lax.dot_general(
        one_hot,
        offset_grad,
        (((0,), (1,)), ((), ())),
        precision=HIGHEST,
        preferred_element_type=jnp.float32,
    )
    def scatter(partial_sum, axis):
        low = partial_sum.astype(jnp.bfloat16)
        return lax.psum_scatter(low, both, scatter_dimension=axis, tiled=True).astype(jnp.float32)

    inner_grad = jnp.stack([scatter(inner_part, 0) for inner_part in inner_sum])
    outer_grad = scatter(outer_sum, 1)
    qkv_out = scatter(jnp.concatenate([qkv_sum, out_sum], axis=1), 0)
    qkv_weight_grad = qkv_out[:, : 3 * model_width]
    out_weight_grad = qkv_out[:, 3 * model_width :]
    small = jnp.concatenate(
        [
            first_gain_sum,
            second_gain_sum,
            jnp.transpose(router_sum).reshape(-1),
            table_part.reshape(-1),
        ]
    )
    small = lax.psum(small.reshape(-1, 128), both).reshape(-1)
    own_rows = attn_gain.shape[0]
    first_own = (lax.axis_index("dp") * lax.axis_size("fsdp") + lax.axis_index("fsdp")) * own_rows
    columns = small[: (2 + experts) * model_width].reshape(2 + experts, model_width)
    columns = lax.dynamic_slice_in_dim(columns, first_own, own_rows, 1)
    attn_gain_grad = columns[0]
    ffn_gain_grad = columns[1]
    router_grad = jnp.transpose(columns[2:])
    table_grad = small[(2 + experts) * model_width :].reshape(bucket_count, head_count)
    return (
        mixed,
        tokens_grad,
        attn_gain_grad,
        qkv_weight_grad,
        out_weight_grad,
        ffn_gain_grad,
        router_grad,
        inner_grad,
        outer_grad,
        table_grad,
    )


def solution(mesh):
    placed = (
        P(("dp", "fsdp"), None),
        P(("dp", "fsdp")),
        P(("dp", "fsdp"), None),
        P(("dp", "fsdp"), None),
        P(("dp", "fsdp")),
        P(("dp", "fsdp"), None),
        P(None, ("dp", "fsdp"), None),
        P(None, ("dp", "fsdp"), None),
        P(),
        P(("dp", "fsdp"), None),
        P(("dp", "fsdp"), None),
        P(),
        P(("dp", "fsdp"), None),
    )
    return jax.shard_map(
        per_device,
        mesh=mesh,
        in_specs=placed,
        out_specs=(
            P(("dp", "fsdp"), None),
            P(("dp", "fsdp"), None),
            P(("dp", "fsdp")),
            P(("dp", "fsdp"), None),
            P(("dp", "fsdp"), None),
            P(("dp", "fsdp")),
            P(("dp", "fsdp"), None),
            P(None, ("dp", "fsdp"), None),
            P(None, ("dp", "fsdp"), None),
            P(),
        ),
        check_vma=False,
    )
```

time: 1810 us -> 920 us (0.51)
  local copies, waits for them, and re-layouts: 616 us -> 16 us
  waiting for transfers between devices: 802 us -> 655 us
  blocking collectives: 121 us -> 40 us
  matrix products: 170 us -> 112 us
  Pallas kernels: 0 us -> 36.8 us
  other arithmetic: 54.2 us -> 35.3 us
    unnamed x7, waiting for transfers between devices: 610 us -> 1.46 us
    reduce_scatter x1 -> x4, waiting for transfers between devices: 192 us -> 439 us  [scatter(): lax.psum_scatter(low, both, scatter_dimension=axis, tiled=True)]
    all_gather x4 -> x3, waiting for transfers between devices: 0.05 us -> 215 us  [the longest x1 94.3 us: per_device(): inner_full = lax.all_gather(inner_weight, both, axis=1, tiled=True)]
    reshape x23 -> x6, local copies, waits for them, and re-layouts: 152 us -> 0.31 us  [the longest x1 0.11 us: per_device(): table_part.reshape(-1)]
    concatenate x13 -> x2, local copies, waits for them, and re-layouts: 114 us -> 1.7 us  [the longest x1 1.65 us: per_device(): jnp.concatenate([qkv_weight, out_weight, attn_gain[:, None], ffn_gain[:,...]
    while x109 -> x0, local copies, waits for them, and re-layouts: 112 us -> none
    slice x35 -> x5, local copies, waits for them, and re-layouts: 107 us -> 3.22 us  [the longest x1 1.6 us: per_device(): qkv_weight_grad = qkv_out[:, :3 * model_width]]
    dot_general x44 -> x3, matrix products: 83.3 us -> 14.1 us  [the longest x1 10.6 us: per_device(): jnp.einsum('ecf,ecd->efd', activated, slot_grad, preferred_element_type=j...]
  transfers between devices with their start and end apart: 6 -> 7, of which waited for: 2 -> 7; matrix products, arithmetic and copies ran while one was open for 16% -> 10% of each run, Pallas kernels for 0% -> 2%
where the time goes in v1:
time: 920 us; the launch traced here: 911 us
  waiting for transfers between devices  655 us (71%)
  matrix products  112 us (12%)
  blocking collectives  40 us (4%)
  Pallas kernels  36.8 us (4%)
  other arithmetic  35.3 us (4%)
  local copies, waits for them, and re-layouts  16 us (2%)
  between operations  15 us (2%)
    reduce_scatter x4, waiting for transfers between devices, scatter(): lax.psum_scatter(low, both, scatter_dimension=axis, tiled=True)  439 us
    all_gather x1, waiting for transfers between devices, per_device(): inner_full = lax.all_gather(inner_weight, both, axis=1, tiled=True)  94.3 us
    all_gather x1, waiting for transfers between devices, per_device(): outer_full = lax.all_gather(outer_weight, both, axis=1, tiled=True)  61 us
    all_gather x1, waiting for transfers between devices, per_device(): packed_full = lax.all_gather(packed, both, axis=0, tiled=True)  59.5 us
    psum x1, blocking collectives, per_device(): small = lax.psum(small.reshape(-1, 128), both).reshape(-1)  40 us
    dot_general x8, matrix products, contract_rows(): lax.dot_general(left_side, right_side, (((0,), (0,)), ((), ())), preferre...  27.9 us
    pallas_call x1, Pallas kernels, attend_forward(): pl.pallas_call(forward_kernel, grid=(groups,), in_specs=[col(0), col(1),...  19.7 us
  transfers between devices with their start and end apart: 7, of which 7 were waited for; matrix products, arithmetic and copies ran while one was open for 10% of the time, Pallas kernels for 2%

profile of v1, /device:TPU:0, one launch (start us, length us, event | category | flops | bytes accessed | tf_op | source)
XLA Modules:
  0.0 910.7 jit_solution(11005069548962181180)
XLA Ops:
  9.6 1.6 concatenate.13
  15.9 1.1 convolution_bitcast_fusion
  19.0 59.5 %all-gather.4.cloned.1.call-done = bf16[768,3200]{1,0:T(8,128)(2,1)} async-done(((bf16[24,3200]{1,0:T(8,128)(2,1)}), bf16[768,3200]{1,0:T(8,128)(2,1)}) %all-gather.4.cloned.1.call-update) | async-done | bytes 4915216 | tf_op jit(solution)/shard_map/all_gather | solution.py:191
  78.5 1.4 convert_reduce_fusion
  80.0 4.1 convolution_convert_fusion.4.query_ref.key_ref.value_ref
  84.1 19.7 %shard_map.204 = (bf16[512,768]{1,0:T(8,128)(2,1)S(1)}, f32[12,512,512]{2,1,0:T(8,128)}) custom-call(bf16[512,2304]{1,0:T(8,128)(2,1)S(1)} %convolution_convert_fusion.4.query_ref.key_ref.value_ref, bf16[512,2304]{1,0:T(8,128)(2,1)S(1)} %convolution_convert_fusion.4.query_ref.key_ref.value_ref, ...), custom_call_target="tpu_custom_call" | custom-call | flops 1610612736 | bytes 16777216 | tf_op jit(solution)/shard_map/pallas_call | solution.py:69
  103.8 2.2 multiply_reduce_fusion.2
  106.0 1.1 copy-done.4
  107.3 1.6 fusion.65
  108.9 1.6 convolution_convert_fusion.7
  110.6 94.3 %all-gather.6.cloned.1.call-done = bf16[2,768,6144]{2,1,0:T(8,128)(2,1)} async-done(((bf16[2,24,6144]{2,1,0:T(8,128)(2,1)}), bf16[2,768,6144]{2,1,0:T(8,128)(2,1)}) %all-gather.6.cloned.1.call-update) | async-done | bytes 18874384 | tf_op jit(solution)/shard_map/all_gather | solution.py:197
  204.9 13.6 %fusion.66 = f32[2,320,6144]{2,1,0:T(8,128)} fusion(bf16[2,320,768]{2,1,0:T(8,128)(2,1)} %bitcast.74, bf16[2,768,6144]{2,1,0:T(8,128)(2,1)} %all-gather.6.cloned.1.call-done), kind=kOutput, calls=%fused_computation.128 | convolution fusion | flops 6039797760 | bytes 35586048 | tf_op jit(solution)/shard_map/ecd,edf->ecf/dot_general | solution.py:252
  218.5 8.5 multiply_convert_fusion
  227.0 61.0 %all-gather.8.cloned.1.call-done = bf16[2,3072,768]{2,1,0:T(8,128)(2,1)} async-done(((bf16[2,96,768]{2,1,0:T(8,128)(2,1)}), bf16[2,3072,768]{2,1,0:T(8,128)(2,1)}) %all-gather.8.cloned.1.call-update) | async-done | bytes 9437200 | tf_op jit(solution)/shard_map/all_gather | solution.py:198
  288.0 8.1 fusion.67
  296.4 0.9 fusion.24
  297.5 2.1 fusion.19
  299.7 1.8 convolution_convert_fusion.6
  301.5 15.7 %fusion.9 = (f32[2,320,3072]{2,1,0:T(8,128)}, f32[2,320,3072]{2,1,0:T(8,128)}) fusion(f32[2,320,6144]{2,1,0:T(8,128)} %fusion.66, bf16[2,320,768]{2,1,0:T(8,128)(2,1)} %bitcast.88, bf16[2,3072,768]{2,1,0:T(8,128)(2,1)} %all-gather.8.cloned.1.call-done), kind=kOutput, calls=%fused_computation.31 | convolution fusion | flops 3063152640 | bytes 41877504 | tf_op jit(solution)/shard_map/ecd,efd->ecf/dot_general | solution.py:269
  317.2 8.7 add_convert_fusion
  325.9 12.5 %fusion.68 = f32[2,320,768]{2,1,0:T(8,128)S(1)} fusion(bf16[2,320,6144]{2,1,0:T(8,128)(2,1)} %add_convert_fusion, bf16[2,768,6144]{2,1,0:T(8,128)(2,1)} %all-gather.6.cloned.1.call-done), kind=kOutput, calls=%fused_computation.130 | convolution fusion | flops 6039797760 | bytes 28704768 | tf_op jit(solution)/shard_map/ecf,edf->ecd/dot_general | solution.py:275
  338.7 0.9 fusion.23
  339.6 1.9 fusion.45
  341.5 1.4 multiply_reduce_fusion
  343.6 1.4 convert_add_fusion.1
  345.0 0.9 convolution_convert_fusion.5
  345.9 2.1 convolution_convert_fusion.8.grad_ref
  348.0 17.2 %shard_map.205 = (bf16[512,768]{1,0:T(8,128)(2,1)S(1)}, bf16[512,768]{1,0:T(8,128)(2,1)S(1)}, bf16[512,768]{1,0:T(8,128)(2,1)S(1)}, f32[6,2,1024]{2,1,0:T(2,128)S(1)}) custom-call(bf16[512,2304]{1,0:T(8,128)(2,1)S(1)} %convolution_convert_fusion.4.query_ref.key_ref.value_ref, bf16[512,2304]{1,0:T(8,128)(2,1)S(1)} %convolution_convert_fusion.4.query_ref.key_ref.value_ref, ...), custom_call_target="tpu_custom_call" | custom-call | flops 4831838208 | bytes 16777216 | tf_op jit(solution)/shard_map/pallas_call | solution.py:139
  365.4 0.9 copy-done.14
  366.3 2.2 convolution_convert_fusion.3
  368.5 2.8 pad_maximum_fusion
  371.4 1.1 copy-done.9
  372.5 9.9 %convolution_convert_fusion = bf16[768,6144]{1,0:T(8,128)(2,1)} fusion(bf16[2,320,6144]{2,1,0:T(8,128)(2,1)} %add_convert_fusion, bf16[640,768]{1,0:T(8,128)(2,1)S(1)} %copy-done.9), kind=kOutput, calls=%fused_computation.3 | convolution fusion | flops 3024617472 | bytes 13860864 | tf_op jit(solution)/shard_map/dot_general | solution.py:29
  382.4 9.7 %convolution_convert_fusion.1 = bf16[768,6144]{1,0:T(8,128)(2,1)} fusion(bf16[2,320,6144]{2,1,0:T(8,128)(2,1)} %add_convert_fusion, bf16[640,768]{1,0:T(8,128)(2,1)S(1)} %copy-done.9), kind=kOutput, calls=%fused_computation.4 | convolution fusion | flops 3024617472 | bytes 13860864 | tf_op jit(solution)/shard_map/dot_general | solution.py:29
  392.2 1.2 copy-done.18
  393.4 10.6 %convolution_convert_fusion.2 = bf16[2,3072,768]{2,1,0:T(8,128)(2,1)} fusion(bf16[2,320,3072]{2,1,0:T(8,128)(2,1)} %multiply_convert_fusion, bf16[2,320,768]{2,1,0:T(8,128)(2,1)S(1)} %bitcast.89), kind=kOutput, calls=%fused_computation.13 | convolution fusion | flops 3024617472 | bytes 14352384 | tf_op jit(solution)/shard_map/ecf,ecd->efd/dot_general | solution.py:268
  404.0 1.1 copy-done.7
  406.3 6.3 fusion.17
  412.6 40.0 %psum.7 = f32[27,128]{1,0:T(8,128)S(1)} all-reduce(f32[27,128]{1,0:T(8,128)S(1)} %maximum_bitcast_fusion), channel_id=1, replica_groups=mesh['dp'=8,'fsdp'=4] {'dp','fsdp'}, use_global_device_ids=true, to_apply=%region_16.17 | all-reduce | flops 3456 | bytes 27648 | tf_op jit(solution)/shard_map/psum | solution.py:337
  454.5 3.0 fusion.20
  457.5 20.7 %reduce-scatter.5.cloned.1.call-done = bf16[24,3072]{1,0:T(8,128)(2,1)} async-done(((bf16[768,3072]{1,0:T(8,128)(2,1)}), bf16[24,3072]{1,0:T(8,128)(2,1)}) %reduce-scatter.5.cloned.1.call-update) | async-done | bytes 147472 | tf_op jit(solution)/shard_map/reduce_scatter | solution.py:322
  478.2 1.4 slice.106
  479.6 1.6 slice.105
  481.2 138.2 %reduce-scatter.9.cloned.1.call-done = bf16[24,6144]{1,0:T(8,128)(2,1)} async-done(((bf16[768,6144]{1,0:T(8,128)(2,1)}), bf16[24,6144]{1,0:T(8,128)(2,1)}) %reduce-scatter.9.cloned.1.call-update) | async-done | bytes 294928 | tf_op jit(solution)/shard_map/reduce_scatter | solution.py:322
  619.4 140.6 %reduce-scatter.7.cloned.1.call-done = bf16[24,6144]{1,0:T(8,128)(2,1)} async-done(((bf16[768,6144]{1,0:T(8,128)(2,1)}), bf16[24,6144]{1,0:T(8,128)(2,1)}) %reduce-scatter.7.cloned.1.call-update) | async-done | bytes 294928 | tf_op jit(solution)/shard_map/reduce_scatter | solution.py:322
  760.0 2.1 maximum_convert_fusion
  762.2 139.4 %reduce-scatter.11.cloned.1.call-done = bf16[2,96,768]{2,1,0:T(8,128)(2,1)} async-done(((bf16[2,3072,768]{2,1,0:T(8,128)(2,1)}), bf16[2,96,768]{2,1,0:T(8,128)(2,1)}) %reduce-scatter.11.cloned.1.call-update) | async-done | bytes 294928 | tf_op jit(solution)/shard_map/reduce_scatter | solution.py:322
  901.6 1.8 convert_element_type.142
  (92 shorter events, 14.1 us)
Async XLA Ops:
  7.2 8.7 copy-start
  7.2 11.8 %copy-start.16 = (s32[512,1]{0,1:T(1,128)S(1)}, s32[512,1]{0,1:T(1,128)}, u32[]{:S(2)}) copy-start(s32[512,1]{0,1:T(1,128)} %param.23) | copy-start | bytes 6148
  7.2 11.6 %copy-start.12 = (bf16[512,768]{1,0:T(8,128)(2,1)S(1)}, bf16[512,768]{1,0:T(8,128)(2,1)}, u32[]{:S(2)}) copy-start(bf16[512,768]{1,0:T(8,128)(2,1)} %param.13) | copy-start | bytes 2359300
  7.2 71.3 %all-gather.4.cloned.1.call-start = ((), (), s32[]{:S(2)}) async-start(), calls=%async_computation.4 | async-start | bytes 5068800 | tf_op jit(solution)/shard_map/all_gather | solution.py:191
  11.2 193.6 %all-gather.6.cloned.1.call-start = ((), (), s32[]{:S(2)}) async-start(), calls=%async_computation.5 | async-start | bytes 19464192 | tf_op jit(solution)/shard_map/all_gather | solution.py:197
  12.0 276.0 %all-gather.8.cloned.1.call-start = ((), (), s32[]{:S(2)}) async-start(), calls=%async_computation.6 | async-start | bytes 9732096 | tf_op jit(solution)/shard_map/all_gather | solution.py:198
  12.7 465.5 %reduce-scatter.5.cloned.1.call-start = ((), (), s32[]{:S(2)}) async-start(), calls=%async_computation.7 | async-start | bytes 4866048 | tf_op jit(solution)/shard_map/reduce_scatter | solution.py:322
  84.1 19.7 %copy-start.13 = (bf16[512,768]{1,0:T(8,128)(2,1)S(1)}, bf16[512,768]{1,0:T(8,128)(2,1)}, u32[]{:S(2)}) copy-start(bf16[512,768]{1,0:T(8,128)(2,1)} %param.13) | copy-start | bytes 2359300
  105.9 1.1 copy-start.4
  107.3 1.6 copy-start.6
  296.4 1.1 copy-start.10
  338.6 2.8 copy-start.5
  341.5 2.1 copy-start.8
  341.5 2.1 copy-start.11
  345.0 3.0 copy-start.2
  365.2 1.1 copy-start.14
  366.3 2.2 copy-start.15
  371.3 1.2 copy-start.9
  371.3 248.1 %reduce-scatter.9.cloned.1.call-start = ((), (), s32[]{:S(2)}) async-start(), calls=%async_computation.9 | async-start | bytes 9732096 | tf_op jit(solution)/shard_map/reduce_scatter | solution.py:322
  382.4 377.6 %reduce-scatter.7.cloned.1.call-start = ((), (), s32[]{:S(2)}) async-start(), calls=%async_computation.8 | async-start | bytes 9732096 | tf_op jit(solution)/shard_map/reduce_scatter | solution.py:322
  392.1 1.2 copy-start.18
  392.2 509.4 %reduce-scatter.11.cloned.1.call-start = ((), (), s32[]{:S(2)}) async-start(), calls=%async_computation.10 | async-start | bytes 9732096 | tf_op jit(solution)/shard_map/reduce_scatter | solution.py:322
  404.0 1.1 copy-start.7
  404.0 1.6 copy-start.17
  406.3 48.2 %copy-start.3 = (f32[512,768]{1,0:T(8,128)S(1)}, f32[512,768]{1,0:T(8,128)}, u32[]{:S(2)}) copy-start(f32[512,768]{1,0:T(8,128)} %copy-done.2) | copy-start | bytes 4718596
  454.5 448.9 %copy-start.1 = (f32[32,12]{0,1:T(8,128)S(1)}, f32[32,12]{0,1:T(8,128)}, u32[]{:S(2)}) copy-start(f32[32,12]{0,1:T(8,128)} %param.21) | copy-start | bytes 4612
Sparse Core Ops, SparseCore 0:
  11.5 67.0 all-gather.3
  81.4 123.4 all-gather.5
  207.7 80.2 all-gather.7
  371.4 106.7 reduce-scatter.4
  484.9 134.4 reduce-scatter.8
  625.2 134.7 reduce-scatter.6
  766.9 134.6 reduce-scatter.10

commit v2 on v1

--- a/solution.py
+++ b/solution.py
@@ -155,6 +155,67 @@
     )(projected, projected, projected, context_grad, weights)
 
 
+def device_bits():
+    bits = []
+    for axis in ("dp", "fsdp"):
+        span = lax.axis_size(axis) // 2
+        while span:
+            bits.append((axis, span))
+            span //= 2
+    return bits
+
+
+def swap_bit(values, bit):
+    axis, span = bit
+    pairs = [(source, source ^ span) for source in range(lax.axis_size(axis))]
+    return lax.ppermute(values, axis, pairs)
+
+
+def own_bit(bit):
+    axis, span = bit
+    return (lax.axis_index(axis) // span) % 2
+
+
+def stage_order(turn):
+    bits = device_bits()
+    outer = list(range(len(bits) - 1))
+    first = {0: ("fsdp", 2), 1: ("dp", 1), 2: ("dp", 2), 3: ("dp", 1)}[turn]
+    begin = bits.index(first) if first in bits else 0
+    order = [(begin - step) % len(outer) for step in range(len(outer))]
+    return [len(bits) - 1] + order
+
+
+def halving_sum(partial_sum, turn):
+
+    bits = device_bits()
+    tail = partial_sum.shape[1:]
+    values = partial_sum.reshape([2] * len(bits) + list(tail))
+    order = stage_order(turn)
+    for place in order:
+        side = own_bit(bits[place])
+        sent = lax.dynamic_slice_in_dim(values, 1 - side, 1, place)
+        kept = lax.dynamic_slice_in_dim(values, side, 1, place)
+        got = swap_bit(sent, bits[place])
+        values = kept.astype(jnp.float32) + got.astype(jnp.float32)
+        if place != order[-1]:
+            values = values.astype(jnp.bfloat16)
+    return values.reshape(tail)
+
+
+def doubling_gather(own, turn):
+
+    bits = device_bits()
+    experts, rows, columns = own.shape
+    values = own.reshape([experts] + [1] * len(bits) + [rows, columns])
+    for place in reversed(stage_order(turn)):
+        side = own_bit(bits[place])
+        got = swap_bit(values, bits[place])
+        lower = jnp.where(side == 0, values, got)
+        upper = jnp.where(side == 0, got, values)
+        values = jnp.concatenate([lower, upper], axis=1 + place)
+    return values.reshape(experts, -1, columns)
+
+
 def per_device(
     tokens,
     attn_gain,
@@ -177,6 +238,7 @@
     experts = inner_weight.shape[0]
     capacity = CAP
     both = ("dp", "fsdp")
+    devices = lax.axis_size("dp") * lax.axis_size("fsdp")
     packed = jnp.concatenate(
         [
             qkv_weight,
@@ -195,7 +257,7 @@
     gains_second = packed_full[:, 4 * model_width + 1]
     router_full = packed_full[:, 4 * model_width + 2 : 4 * model_width + 2 + experts]
     inner_full = lax.all_gather(inner_weight, both, axis=1, tiled=True)
-    outer_full = lax.all_gather(outer_weight, both, axis=1, tiled=True)
+    outer_full = doubling_gather(outer_weight, 0)
     hidden_width = outer_full.shape[1]
     position = jnp.arange(row_count, dtype=jnp.int32)
     seq_ends = jnp.cumsum(lengths[0])
@@ -272,6 +334,18 @@
     inner_sum = [
         contract_rows(expert_rows[expert], gate_up_grad[expert]) for expert in range(experts)
     ]
+    def by_owner(partial_sum):
+        return partial_sum.astype(jnp.bfloat16).reshape(devices, -1, partial_sum.shape[-1])
+
+    outer_low = jnp.concatenate(
+        [outer_sum[expert].astype(jnp.bfloat16).reshape(devices, -1, model_width) for expert in range(experts)],
+        axis=1,
+    )
+    outer_grad = halving_sum(outer_low, 0).reshape(experts, -1, model_width)
+    inner_low = [by_owner(inner_part) for inner_part in inner_sum]
+    inner_grad = jnp.stack(
+        [halving_sum(inner_low[expert], 1 + expert % 2) for expert in range(experts)]
+    )
     rows_grad = jnp.einsum(
         "ecf,edf->ecd", gate_up_grad, inner_full, preferred_element_type=jnp.float32
     )
@@ -297,6 +371,7 @@
     middle_part, second_gain_sum = norm_two_pull(normed_two_grad)
     middle_grad = cotangent + middle_part
     attended_grad = (live_rows * middle_grad).astype(jnp.bfloat16)
+    attended_grad, *_ = lax.optimization_barrier((attended_grad, outer_low, *inner_low))
     out_sum = contract_rows(context, attended_grad)
     context_grad = contract_cols(attended_grad, out_full).astype(jnp.bfloat16)
 
@@ -317,13 +392,7 @@
         precision=HIGHEST,
         preferred_element_type=jnp.float32,
     )
-    def scatter(partial_sum, axis):
-        low = partial_sum.astype(jnp.bfloat16)
-        return lax.psum_scatter(low, both, scatter_dimension=axis, tiled=True).astype(jnp.float32)
-
-    inner_grad = jnp.stack([scatter(inner_part, 0) for inner_part in inner_sum])
-    outer_grad = scatter(outer_sum, 1)
-    qkv_out = scatter(jnp.concatenate([qkv_sum, out_sum], axis=1), 0)
+    qkv_out = halving_sum(by_owner(jnp.concatenate([qkv_sum, out_sum], axis=1)), 3)
     qkv_weight_grad = qkv_out[:, : 3 * model_width]
     out_weight_grad = qkv_out[:, 3 * model_width :]
     small = jnp.concatenate(

time: 920 us -> 661 us (0.72)
  waiting for transfers between devices: 655 us -> 313 us
  other arithmetic: 35.3 us -> 83.3 us
  local copies, waits for them, and re-layouts: 16 us -> 45.1 us
  starting transfers between devices: 0.28 us -> 19.6 us
  matrix products: 112 us -> 101 us
    reduce_scatter x4 -> x0, waiting for transfers between devices: 439 us -> none  [scatter(): lax.psum_scatter(low, both, scatter_dimension=axis, tiled=True)]
    ppermute x0 -> x25, waiting for transfers between devices: none -> 310 us  [swap_bit(): return lax.ppermute(values, axis, pairs)]
    all_gather x1, waiting for transfers between devices: 94.3 us -> 2.61 us  [per_device(): inner_full = lax.all_gather(inner_weight, both, axis=1, tiled=True)]
    all_gather x1 -> x0, waiting for transfers between devices: 61 us -> none  [per_device(): outer_full = lax.all_gather(outer_weight, both, axis=1, tiled=True)]
    all_gather x1, waiting for transfers between devices: 59.5 us -> 0.01 us  [per_device(): packed_full = lax.all_gather(packed, both, axis=0, tiled=True)]
    convert_element_type x1 -> x17, other arithmetic: 1.81 us -> 28.8 us  [the longest x16 28.3 us: halving_sum(): values = values.astype(jnp.bfloat16)]
    ppermute x0 -> x25, starting transfers between devices: none -> 19.5 us  [swap_bit(): return lax.ppermute(values, axis, pairs)]
    select_n x0 -> x5, other arithmetic: none -> 12.3 us  [doubling_gather(): lower = jnp.where(side == 0, values, got)]
  transfers between devices with their start and end apart: 7 -> 27, of which waited for: 7 -> 18; matrix products, arithmetic and copies ran while one was open for 10% -> 17% of each run, Pallas kernels for 2% -> 3%
where the time goes in v2:
time: 661 us; the launch traced here: 657 us
  waiting for transfers between devices  313 us (47%)
  matrix products  101 us (15%)
  other arithmetic  83.3 us (13%)
  local copies, waits for them, and re-layouts  45.1 us (7%)
  blocking collectives  42.7 us (6%)
  Pallas kernels  37 us (6%)
  starting transfers between devices  19.6 us (3%)
  between operations  15.4 us (2%)
    ppermute x25, waiting for transfers between devices, swap_bit(): return lax.ppermute(values, axis, pairs)  310 us
    psum x1, blocking collectives, per_device(): small = lax.psum(small.reshape(-1, 128), both).reshape(-1)  42.7 us
    convert_element_type x16, other arithmetic, halving_sum(): values = values.astype(jnp.bfloat16)  28.3 us
    dot_general x8, matrix products, contract_rows(): lax.dot_general(left_side, right_side, (((0,), (0,)), ((), ())), preferre...  23.2 us
    pallas_call x1, Pallas kernels, attend_forward(): pl.pallas_call(forward_kernel, grid=(groups,), in_specs=[col(0), col(1),...  19.7 us
    ppermute x25, starting transfers between devices, swap_bit(): return lax.ppermute(values, axis, pairs)  19.5 us
    pallas_call x1, Pallas kernels, attend_backward(): pl.pallas_call(backward_kernel, grid=(groups,), in_specs=[col(0), col(1),...  17.4 us
    dot_general x1, matrix products, per_device(): jnp.einsum('ecd,efd->ecf', slot_grad, outer_full, preferred_element_type=...  15.9 us
  transfers between devices with their start and end apart: 27, of which 18 were waited for; matrix products, arithmetic and copies ran while one was open for 17% of the time, Pallas kernels for 3%

profile of v2, /device:TPU:0, one launch (start us, length us, event | category | flops | bytes accessed | tf_op | source)
XLA Modules:
  0.0 657.4 jit_solution(583239277315942606)
XLA Ops:
  11.9 4.1 collective-permute-start
  16.0 15.5 %collective-permute-done = bf16[2,1,1,1,1,1,96,768]{7,6,0,5,4,3,2,1:T(8,128)(2,1)S(1)} collective-permute-done((bf16[2,1,1,1,1,1,96,768]{7,6,0,5,4,3,2,1:T(8,128)(2,1)}, bf16[2,1,1,1,1,1,96,768]{7,6,0,5,4,3,2,1:T(8,128)(2,1)S(1)}, u32[]{:S(2)}, u32[]{:S(2)}) %collective-permute-start) | collective-permute-done | bytes 294944 | tf_op jit(solution)/shard_map/ppermute | solution.py:171
  33.9 18.0 %collective-permute-done.1 = bf16[2,2,1,1,1,1,96,768]{7,6,0,5,4,3,2,1:T(8,128)(2,1)S(1)} collective-permute-done((bf16[2,2,1,1,1,1,96,768]{7,6,0,5,4,3,2,1:T(8,128)(2,1)S(1)}, bf16[2,2,1,1,1,1,96,768]{7,6,0,5,4,3,2,1:T(8,128)(2,1)S(1)}, u32[]{:S(2)}, u32[]{:S(2)}) %collective-permute-start.1) | collective-permute-done | bytes 589856 | tf_op jit(solution)/shard_map/ppermute | solution.py:171
  53.5 32.7 %collective-permute-done.2 = bf16[2,2,2,1,1,1,96,768]{7,6,0,5,4,3,2,1:T(8,128)(2,1)S(1)} collective-permute-done((bf16[2,2,2,1,1,1,96,768]{7,6,0,5,4,3,2,1:T(8,128)(2,1)S(1)}, bf16[2,2,2,1,1,1,96,768]{7,6,0,5,4,3,2,1:T(8,128)(2,1)S(1)}, u32[]{:S(2)}, u32[]{:S(2)}) %collective-permute-start.2) | collective-permute-done | bytes 1179680 | tf_op jit(solution)/shard_map/ppermute | solution.py:171
  88.6 61.4 %collective-permute-done.3 = bf16[2,2,2,2,1,1,96,768]{7,6,0,5,4,3,2,1:T(8,128)(2,1)} collective-permute-done((bf16[2,2,2,2,1,1,96,768]{7,6,0,5,4,3,2,1:T(8,128)(2,1)S(1)}, bf16[2,2,2,2,1,1,96,768]{7,6,0,5,4,3,2,1:T(8,128)(2,1)}, u32[]{:S(2)}, u32[]{:S(2)}) %collective-permute-start.3) | collective-permute-done | bytes 2359328 | tf_op jit(solution)/shard_map/ppermute | solution.py:171
  150.0 2.4 broadcast_select_fusion.3
  152.5 2.6 pad_maximum_fusion.1
  159.2 4.4 collective-permute-done.4
  163.6 8.6 %broadcast_select_fusion.1 = (bf16[2,2,2,2,2,1,96,768]{7,6,0,5,4,3,2,1:T(8,128)(2,1)}, bf16[2,2,2,2,2,1,96,768]{7,6,0,5,4,3,2,1:T(8,128)(2,1)}) fusion(bf16[2,2,2,2,2,1,96,768]{7,6,0,5,4,3,2,1:T(8,128)(2,1)} %collective-permute-done.4, pred[]{:T(512)S(6)} %eq.111, bf16[2,2,2,2,1,1,96,768]{7,6,0,5,4,3,2,1:T(8,128)(2,1)} %copy-done.6, ...), kind=kLoop, calls=%fused_computation.35 | loop fusion | flops 7077888 | bytes 18874368 | tf_op jit(solution)/shard_map/jit(_where)/select_n | solution.py:213
  172.3 8.3 %pad_maximum_fusion = bf16[2,2,2,2,2,2,96,768]{7,6,0,5,4,3,2,1:T(8,128)(2,1)} fusion(bf16[2,2,2,2,2,1,96,768]{7,6,0,5,4,3,2,1:T(8,128)(2,1)} %get-tuple-element.56, bf16[2,2,2,2,2,1,96,768]{7,6,0,5,4,3,2,1:T(8,128)(2,1)} %get-tuple-element.55), kind=kLoop, calls=%fused_computation.9 | loop fusion | flops 4718592 | bytes 18874368 | tf_op jit(solution)/shard_map/concatenate | solution.py:215
  180.6 8.1 %copy.38 = bf16[2,2,2,2,2,2,96,768]{7,6,5,4,3,2,1,0:T(8,128)(2,1)} copy(bf16[2,2,2,2,2,2,96,768]{7,6,0,5,4,3,2,1:T(8,128)(2,1)} %pad_maximum_fusion) | data formatting | bytes 18874368 | tf_op jit(solution)/shard_map/concatenate | solution.py:215
  190.0 4.1 convolution_convert_fusion.4.query_ref.key_ref.value_ref
  194.1 19.7 %shard_map.204 = (bf16[512,768]{1,0:T(8,128)(2,1)S(1)}, f32[12,512,512]{2,1,0:T(8,128)}) custom-call(bf16[512,2304]{1,0:T(8,128)(2,1)S(1)} %convolution_convert_fusion.4.query_ref.key_ref.value_ref, bf16[512,2304]{1,0:T(8,128)(2,1)S(1)} %convolution_convert_fusion.4.query_ref.key_ref.value_ref, ...), custom_call_target="tpu_custom_call" | custom-call | flops 1610612736 | bytes 16777216 | tf_op jit(solution)/shard_map/pallas_call | solution.py:69
  220.6 2.6 all-gather.5.cloned.1.call-done
  223.2 13.6 %fusion.71 = f32[2,320,6144]{2,1,0:T(8,128)} fusion(bf16[2,320,768]{2,1,0:T(8,128)(2,1)} %bitcast.111, bf16[2,768,6144]{2,1,0:T(8,128)(2,1)} %all-gather.5.cloned.1.call-done), kind=kOutput, calls=%fused_computation.193 | convolution fusion | flops 6039797760 | bytes 35586048 | tf_op jit(solution)/shard_map/ecd,edf->ecf/dot_general | solution.py:314
  236.8 7.3 %multiply_convert_fusion = bf16[2,320,3072]{2,1,0:T(8,128)(2,1)S(1)} fusion(f32[2,320,6144]{2,1,0:T(8,128)} %fusion.71), kind=kLoop, calls=%fused_computation.19 | loop fusion | flops 19660800 | bytes 19660800 | tf_op jit(solution)/shard_map/convert_element_type | solution.py:317
  244.1 5.8 fusion.72
  255.3 7.5 %convolution_convert_fusion.2 = bf16[2,3072,768]{2,1,0:T(8,128)(2,1)} fusion(bf16[2,320,3072]{2,1,0:T(8,128)(2,1)S(1)} %multiply_convert_fusion, bf16[2,320,768]{2,1,0:T(8,128)(2,1)S(1)} %bitcast.125), kind=kOutput, calls=%fused_computation.21 | convolution fusion | flops 3024617472 | bytes 14352384 | tf_op jit(solution)/shard_map/ecf,ecd->efd/dot_general | solution.py:330
  262.8 15.9 %fusion.11 = (f32[2,320,3072]{2,1,0:T(8,128)}, f32[2,320,3072]{2,1,0:T(8,128)}) fusion(f32[2,320,6144]{2,1,0:T(8,128)} %fusion.71, bf16[2,320,768]{2,1,0:T(8,128)(2,1)} %bitcast.126, bf16[2,3072,768]{2,1,0:T(8,128)(2,1)} %bitcast.104), kind=kOutput, calls=%fused_computation.51 | convolution fusion | flops 3063152640 | bytes 41877504 | tf_op jit(solution)/shard_map/ecd,efd->ecf/dot_general | solution.py:331
  278.8 6.5 fusion.69
  285.2 7.9 %add_convert_fusion = bf16[2,320,6144]{2,1,0:T(8,128)(2,1)S(1)} fusion(f32[2,320,3072]{2,1,0:T(8,128)} %get-tuple-element.52, f32[2,320,3072]{2,1,0:T(8,128)} %get-tuple-element.51), kind=kLoop, calls=%fused_computation | loop fusion | flops 7864320 | bytes 23592960 | tf_op jit(solution)/shard_map/convert_element_type | solution.py:333
  293.2 3.2 copy-done.13
  296.3 7.5 %convolution_convert_fusion.1 = bf16[768,6144]{1,0:T(8,128)(2,1)} fusion(bf16[2,320,6144]{2,1,0:T(8,128)(2,1)S(1)} %add_convert_fusion, bf16[640,768]{1,0:T(8,128)(2,1)S(1)} %copy-done.19), kind=kOutput, calls=%fused_computation.8 | convolution fusion | flops 3024617472 | bytes 13860864 | tf_op jit(solution)/shard_map/dot_general | solution.py:29
  303.9 13.2 %fusion.73 = f32[2,320,768]{2,1,0:T(8,128)} fusion(bf16[2,320,6144]{2,1,0:T(8,128)(2,1)} %copy-done.13, bf16[2,768,6144]{2,1,0:T(8,128)(2,1)} %all-gather.5.cloned.1.call-done), kind=kOutput, calls=%fused_computation.195 | convolution fusion | flops 6039797760 | bytes 28704768 | tf_op jit(solution)/shard_map/ecf,edf->ecd/dot_general | solution.py:349
  327.2 17.4 %shard_map.205 = (bf16[512,768]{1,0:T(8,128)(2,1)S(1)}, bf16[512,768]{1,0:T(8,128)(2,1)S(1)}, bf16[512,768]{1,0:T(8,128)(2,1)S(1)}, f32[6,2,1024]{2,1,0:T(2,128)S(1)}) custom-call(bf16[512,2304]{1,0:T(8,128)(2,1)S(1)} %convolution_convert_fusion.4.query_ref.key_ref.value_ref, bf16[512,2304]{1,0:T(8,128)(2,1)S(1)} %convolution_convert_fusion.4.query_ref.key_ref.value_ref, ...), custom_call_target="tpu_custom_call" | custom-call | flops 4831838208 | bytes 16777216 | tf_op jit(solution)/shard_map/pallas_call | solution.py:139
  348.5 2.6 fusion.6
  351.3 5.1 constant_dynamic-slice_fusion.13
  357.1 7.5 %convolution_convert_fusion = bf16[768,6144]{1,0:T(8,128)(2,1)S(1)} fusion(bf16[2,320,6144]{2,1,0:T(8,128)(2,1)} %copy-done.13, bf16[640,768]{1,0:T(8,128)(2,1)S(1)} %copy-done.20), kind=kOutput, calls=%fused_computation.7 | convolution fusion | flops 3024617472 | bytes 13860864 | tf_op jit(solution)/shard_map/dot_general | solution.py:29
  364.6 4.2 add_convert_fusion.7
  372.8 2.6 constant_dynamic-slice_fusion.8
  376.1 6.2 fusion.21
  382.3 17.3 %collective-permute-done.6 = bf16[2,2,1,2,1,24,3072]{6,5,4,3,2,1,0:T(8,128)(2,1)} collective-permute-done((bf16[2,2,1,2,1,24,3072]{6,5,4,3,2,1,0:T(8,128)(2,1)}, bf16[2,2,1,2,1,24,3072]{6,5,4,3,2,1,0:T(8,128)(2,1)}, u32[]{:S(2)}, u32[]{:S(2)}) %collective-permute-start.6) | collective-permute-done | bytes 1179680 | tf_op jit(solution)/shard_map/ppermute | solution.py:171
  403.4 42.7 %psum.7 = f32[27,128]{1,0:T(8,128)S(1)} all-reduce(f32[27,128]{1,0:T(8,128)S(1)} %maximum_bitcast_fusion), channel_id=1, replica_groups=mesh['dp'=8,'fsdp'=4] {'dp','fsdp'}, use_global_device_ids=true, to_apply=%region_16.17 | all-reduce | flops 3456 | bytes 27648 | tf_op jit(solution)/shard_map/psum | solution.py:406
  446.9 4.0 fusion.24
  454.6 13.4 %collective-permute-done.8 = bf16[1,1,1,2,1,24,3072]{6,5,4,3,2,1,0:T(8,128)(2,1)S(1)} collective-permute-done((bf16[1,1,1,2,1,24,3072]{6,5,4,3,2,1,0:T(8,128)(2,1)S(1)}, bf16[1,1,1,2,1,24,3072]{6,5,4,3,2,1,0:T(8,128)(2,1)S(1)}, u32[]{:S(2)}, u32[]{:S(2)}) %collective-permute-start.8) | collective-permute-done | bytes 294944 | tf_op jit(solution)/shard_map/ppermute | solution.py:171
  470.0 3.9 collective-permute-done.9
  475.4 4.0 add_convert_fusion.1
  480.9 5.6 add_convert_fusion.3
  489.5 5.6 add_convert_fusion.2
  495.4 36.6 %collective-permute-done.21 = bf16[2,2,2,1,1,192,768]{6,5,4,3,2,1,0:T(8,128)(2,1)S(1)} collective-permute-done((bf16[2,2,2,1,1,192,768]{6,5,4,3,2,1,0:T(8,128)(2,1)S(1)}, bf16[2,2,2,1,1,192,768]{6,5,4,3,2,1,0:T(8,128)(2,1)S(1)}, u32[]{:S(2)}, u32[]{:S(2)}) %collective-permute-start.21) | collective-permute-done | bytes 2359328 | tf_op jit(solution)/shard_map/ppermute | solution.py:171
  534.0 8.5 %collective-permute-done.11 = bf16[2,2,1,2,1,24,6144]{6,5,4,3,2,1,0:T(8,128)(2,1)} collective-permute-done((bf16[2,2,1,2,1,24,6144]{6,5,4,3,2,1,0:T(8,128)(2,1)}, bf16[2,2,1,2,1,24,6144]{6,5,4,3,2,1,0:T(8,128)(2,1)}, u32[]{:S(2)}, u32[]{:S(2)}) %collective-permute-start.11) | collective-permute-done | bytes 2359328 | tf_op jit(solution)/shard_map/ppermute | solution.py:171
  542.5 2.3 add_convert_fusion.6
  545.0 17.2 %collective-permute-done.16 = bf16[2,1,2,2,1,24,6144]{6,5,4,3,2,1,0:T(8,128)(2,1)S(1)} collective-permute-done((bf16[2,1,2,2,1,24,6144]{6,5,4,3,2,1,0:T(8,128)(2,1)S(1)}, bf16[2,1,2,2,1,24,6144]{6,5,4,3,2,1,0:T(8,128)(2,1)S(1)}, u32[]{:S(2)}, u32[]{:S(2)}) %collective-permute-start.16) | collective-permute-done | bytes 2359328 | tf_op jit(solution)/shard_map/ppermute | solution.py:171
  563.2 2.4 collective-permute-done.22
  566.2 26.4 %collective-permute-done.12 = bf16[2,1,1,2,1,24,6144]{6,5,4,3,2,1,0:T(8,128)(2,1)S(1)} collective-permute-done((bf16[2,1,1,2,1,24,6144]{6,5,4,3,2,1,0:T(8,128)(2,1)S(1)}, bf16[2,1,1,2,1,24,6144]{6,5,4,3,2,1,0:T(8,128)(2,1)S(1)}, u32[]{:S(2)}, u32[]{:S(2)}) %collective-permute-start.12) | collective-permute-done | bytes 1179680 | tf_op jit(solution)/shard_map/ppermute | solution.py:171
  593.1 35.7 %collective-permute-done.17 = bf16[1,1,2,2,1,24,6144]{6,5,4,3,2,1,0:T(8,128)(2,1)S(1)} collective-permute-done((bf16[1,1,2,2,1,24,6144]{6,5,4,3,2,1,0:T(8,128)(2,1)S(1)}, bf16[1,1,2,2,1,24,6144]{6,5,4,3,2,1,0:T(8,128)(2,1)S(1)}, u32[]{:S(2)}, u32[]{:S(2)}) %collective-permute-start.17) | collective-permute-done | bytes 1179680 | tf_op jit(solution)/shard_map/ppermute | solution.py:171
  630.0 10.4 %collective-permute-done.13 = bf16[1,1,1,2,1,24,6144]{6,5,4,3,2,1,0:T(8,128)(2,1)S(1)} collective-permute-done((bf16[1,1,1,2,1,24,6144]{6,5,4,3,2,1,0:T(8,128)(2,1)S(1)}, bf16[1,1,1,2,1,24,6144]{6,5,4,3,2,1,0:T(8,128)(2,1)S(1)}, u32[]{:S(2)}, u32[]{:S(2)}) %collective-permute-start.13) | collective-permute-done | bytes 589856 | tf_op jit(solution)/shard_map/ppermute | solution.py:171
  642.1 5.2 collective-permute-done.14
  (216 shorter events, 74.5 us)
Async XLA Ops:
  7.2 149.2 %copy-start = (f32[32,12]{0,1:T(8,128)S(1)}, f32[32,12]{0,1:T(8,128)}, u32[]{:S(2)}) copy-start(f32[32,12]{0,1:T(8,128)} %param.21) | copy-start | bytes 4612
  7.2 181.5 %all-gather.3.cloned.1.call-start = ((), (), s32[]{:S(2)}) async-start(), calls=%async_computation | async-start | bytes 5068800 | tf_op jit(solution)/shard_map/all_gather | solution.py:253
  11.2 212.1 %all-gather.5.cloned.1.call-start = ((), (), s32[]{:S(2)}) async-start(), calls=%async_computation.1 | async-start | bytes 19464192 | tf_op jit(solution)/shard_map/all_gather | solution.py:259
  11.9 19.6 %collective-permute-start = (bf16[2,1,1,1,1,1,96,768]{7,6,0,5,4,3,2,1:T(8,128)(2,1)}, bf16[2,1,1,1,1,1,96,768]{7,6,0,5,4,3,2,1:T(8,128)(2,1)S(1)}, u32[]{:S(2)}, u32[]{:S(2)}) collective-permute-start(bf16[2,1,1,1,1,1,96,768]{7,6,0,5,4,3,2,1:T(8,128)(2,1)} %bitcast.113), channel_id=1, source_target_pairs={{0,16},{4,20},{8,24},{12,28},{16,0},{20,4},{24,8},{28,12},{1,17},{... | collective-permute-start | bytes 884744 | tf_op jit(solution)/shard_map/ppermute | solution.py:171
  32.6 19.2 %collective-permute-start.1 = (bf16[2,2,1,1,1,1,96,768]{7,6,0,5,4,3,2,1:T(8,128)(2,1)S(1)}, bf16[2,2,1,1,1,1,96,768]{7,6,0,5,4,3,2,1:T(8,128)(2,1)S(1)}, u32[]{:S(2)}, u32[]{:S(2)}) collective-permute-start(bf16[2,2,1,1,1,1,96,768]{7,6,0,5,4,3,2,1:T(8,128)(2,1)S(1)} %pad_maximum_fusion.5), channel_id=1, source_target_pairs={{0,8},{4,12},{8,0},{12,4},{16,24},{20,28},{24,16},{28,20},{1,9},{5... | collective-permute-start | bytes 1769480 | tf_op jit(solution)/shard_map/ppermute | solution.py:171
  52.1 34.2 %collective-permute-start.2 = (bf16[2,2,2,1,1,1,96,768]{7,6,0,5,4,3,2,1:T(8,128)(2,1)S(1)}, bf16[2,2,2,1,1,1,96,768]{7,6,0,5,4,3,2,1:T(8,128)(2,1)S(1)}, u32[]{:S(2)}, u32[]{:S(2)}) collective-permute-start(bf16[2,2,2,1,1,1,96,768]{7,6,0,5,4,3,2,1:T(8,128)(2,1)S(1)} %pad_maximum_fusion.3), channel_id=1, source_target_pairs={{0,4},{4,0},{8,12},{12,8},{16,20},{20,16},{24,28},{28,24},{1,5},{5... | collective-permute-start | bytes 3538952 | tf_op jit(solution)/shard_map/ppermute | solution.py:171
  87.4 62.6 %collective-permute-start.3 = (bf16[2,2,2,2,1,1,96,768]{7,6,0,5,4,3,2,1:T(8,128)(2,1)S(1)}, bf16[2,2,2,2,1,1,96,768]{7,6,0,5,4,3,2,1:T(8,128)(2,1)}, u32[]{:S(2)}, u32[]{:S(2)}) collective-permute-start(bf16[2,2,2,2,1,1,96,768]{7,6,0,5,4,3,2,1:T(8,128)(2,1)S(1)} %pad_maximum_fusion.2), channel_id=1, source_target_pairs={{0,2},{1,3},{2,0},{3,1},{4,6},{5,7},{6,4},{7,5},{8,10},{9,11},{10,... | collective-permute-start | bytes 7077896 | tf_op jit(solution)/shard_map/ppermute | solution.py:171
  152.5 4.0 copy-start.28
  152.5 4.5 copy-start.25
  152.5 6.5 copy-start.21
  155.4 8.3 %collective-permute-start.4 = (bf16[2,2,2,2,2,1,96,768]{7,6,0,5,4,3,2,1:T(8,128)(2,1)}, bf16[2,2,2,2,2,1,96,768]{7,6,0,5,4,3,2,1:T(8,128)(2,1)}, u32[]{:S(2)}, u32[]{:S(2)}) collective-permute-start(bf16[2,2,2,2,2,1,96,768]{7,6,0,5,4,3,2,1:T(8,128)(2,1)} %pad_maximum_fusion.1), channel_id=1, source_target_pairs={{0,1},{1,0},{2,3},{3,2},{4,5},{5,4},{6,7},{7,6},{8,9},{9,8},{10,11... | collective-permute-start | bytes 14155784 | tf_op jit(solution)/shard_map/ppermute | solution.py:171
  159.2 13.1 %copy-start.26 = (f32[512]{0:T(512)}, f32[512]{0:T(512)S(1)}, u32[]{:S(2)}) copy-start(f32[512]{0:T(512)S(1)} %fusion.25) | copy-start | bytes 6148
  194.1 19.7 %copy-start.22 = (bf16[512,768]{1,0:T(8,128)(2,1)S(1)}, bf16[512,768]{1,0:T(8,128)(2,1)}, u32[]{:S(2)}) copy-start(bf16[512,768]{1,0:T(8,128)(2,1)} %param.13) | copy-start | bytes 2359300
  285.2 63.2 %copy-start.2 = (bf16[1,3072,768]{2,1,0:T(8,128)(2,1)}, bf16[1,3072,768]{2,1,0:T(8,128)(2,1)S(1)}, u32[]{:S(2)}) copy-start(bf16[1,3072,768]{2,1,0:T(8,128)(2,1)S(1)} %get-tuple-element.53) | copy-start | bytes 14155780
  285.2 11.1 %copy-start.19 = (bf16[640,768]{1,0:T(8,128)(2,1)S(1)}, bf16[640,768]{1,0:T(8,128)(2,1)}, u32[]{:S(2)}) copy-start(bf16[640,768]{1,0:T(8,128)(2,1)} %convolution_convert_fusion.7) | copy-start | bytes 2949124
  293.2 3.2 copy-start.13
  344.7 3.8 slice-start.2
  348.1 16.5 %collective-permute-start.5 = (bf16[2,2,2,2,1,24,3072]{6,5,4,3,2,1,0:T(8,128)(2,1)S(1)}, bf16[2,2,2,2,1,24,3072]{6,5,4,3,2,1,0:T(8,128)(2,1)}, u32[]{:S(2)}, u32[]{:S(2)}) collective-permute-start(bf16[2,2,2,2,1,24,3072]{6,5,4,3,2,1,0:T(8,128)(2,1)S(1)} %fusion.12), channel_id=1, source_target_pairs={{0,1},{1,0},{2,3},{3,2},{4,5},{5,4},{6,7},{7,6},{8,9},{9,8},{10,11... | collective-permute-start | bytes 7077896 | tf_op jit(solution)/shard_map/ppermute | solution.py:171
  351.1 124.2 %collective-permute-start.20 = (bf16[2,2,2,2,1,192,768]{6,5,4,3,2,1,0:T(8,128)(2,1)}, bf16[2,2,2,2,1,192,768]{6,5,4,3,2,1,0:T(8,128)(2,1)}, u32[]{:S(2)}, u32[]{:S(2)}) collective-permute-start(bf16[2,2,2,2,1,192,768]{6,5,4,3,2,1,0:T(8,128)(2,1)} %fusion.6), channel_id=1, source_target_pairs={{0,1},{1,0},{2,3},{3,2},{4,5},{5,4},{6,7},{7,6},{8,9},{9,8},{10,11... | collective-permute-start | bytes 14155784 | tf_op jit(solution)/shard_map/ppermute | solution.py:171
  351.3 5.4 copy-start.15
  351.3 5.8 copy-start.20
  356.4 124.5 %collective-permute-start.10 = (bf16[2,2,2,2,1,24,6144]{6,5,4,3,2,1,0:T(8,128)(2,1)}, bf16[2,2,2,2,1,24,6144]{6,5,4,3,2,1,0:T(8,128)(2,1)}, u32[]{:S(2)}, u32[]{:S(2)}) collective-permute-start(bf16[2,2,2,2,1,24,6144]{6,5,4,3,2,1,0:T(8,128)(2,1)} %constant_dynamic-slice_fusion.13), channel_id=1, source_target_pairs={{0,1},{1,0},{2,3},{3,2},{4,5},{5,4},{6,7},{7,6},{8,9},{9,8},{10,11... | collective-permute-start | bytes 14155784 | tf_op jit(solution)/shard_map/ppermute | solution.py:171
  364.6 8.2 %copy-start.10 = (bf16[768,6144]{1,0:T(8,128)(2,1)}, bf16[768,6144]{1,0:T(8,128)(2,1)S(1)}, u32[]{:S(2)}) copy-start(bf16[768,6144]{1,0:T(8,128)(2,1)S(1)} %convolution_convert_fusion) | copy-start | bytes 28311556
  371.3 28.3 %collective-permute-start.6 = (bf16[2,2,1,2,1,24,3072]{6,5,4,3,2,1,0:T(8,128)(2,1)}, bf16[2,2,1,2,1,24,3072]{6,5,4,3,2,1,0:T(8,128)(2,1)}, u32[]{:S(2)}, u32[]{:S(2)}) collective-permute-start(bf16[2,2,1,2,1,24,3072]{6,5,4,3,2,1,0:T(8,128)(2,1)} %constant_dynamic-slice_fusion.17), channel_id=1, source_target_pairs={{0,4},{4,0},{8,12},{12,8},{16,20},{20,16},{24,28},{28,24},{1,5},{5... | collective-permute-start | bytes 3538952 | tf_op jit(solution)/shard_map/ppermute | solution.py:171
  375.3 114.2 %collective-permute-start.15 = (bf16[2,2,2,2,1,24,6144]{6,5,4,3,2,1,0:T(8,128)(2,1)}, bf16[2,2,2,2,1,24,6144]{6,5,4,3,2,1,0:T(8,128)(2,1)}, u32[]{:S(2)}, u32[]{:S(2)}) collective-permute-start(bf16[2,2,2,2,1,24,6144]{6,5,4,3,2,1,0:T(8,128)(2,1)} %constant_dynamic-slice_fusion.8), channel_id=1, source_target_pairs={{0,1},{1,0},{2,3},{3,2},{4,5},{5,4},{6,7},{7,6},{8,9},{9,8},{10,11... | collective-permute-start | bytes 14155784 | tf_op jit(solution)/shard_map/ppermute | solution.py:171
  376.1 6.2 copy-start.27
  376.1 23.6 %copy-start.12 = (bf16[2,2,2,2,1,24,3072]{6,5,4,3,2,1,0:T(8,128)(2,1)S(1)}, bf16[2,2,2,2,1,24,3072]{6,5,4,3,2,1,0:T(8,128)(2,1)}, u32[]{:S(2)}) copy-start(bf16[2,2,2,2,1,24,3072]{6,5,4,3,2,1,0:T(8,128)(2,1)} %copy-done.11) | copy-start | bytes 7077892
  382.3 64.5 %copy-start.5 = (f32[512,768]{1,0:T(8,128)S(1)}, f32[512,768]{1,0:T(8,128)}, u32[]{:S(2)}) copy-start(f32[512,768]{1,0:T(8,128)} %copy-done.3) | copy-start | bytes 4718596
  382.3 64.5 %copy-start.8 = (f32[512,768]{1,0:T(8,128)S(1)}, f32[512,768]{1,0:T(8,128)}, u32[]{:S(2)}) copy-start(f32[512,768]{1,0:T(8,128)} %copy-done.7) | copy-start | bytes 4718596
  403.2 47.7 %collective-permute-start.7 = (bf16[2,1,1,2,1,24,3072]{6,5,4,3,2,1,0:T(8,128)(2,1)}, bf16[2,1,1,2,1,24,3072]{6,5,4,3,2,1,0:T(8,128)(2,1)}, u32[]{:S(2)}, u32[]{:S(2)}) collective-permute-start(bf16[2,1,1,2,1,24,3072]{6,5,4,3,2,1,0:T(8,128)(2,1)} %constant_dynamic-slice_fusion.16), channel_id=1, source_target_pairs={{0,8},{4,12},{8,0},{12,4},{16,24},{20,28},{24,16},{28,20},{1,9},{5... | collective-permute-start | bytes 1769480 | tf_op jit(solution)/shard_map/ppermute | solution.py:171
  446.8 28.5 %slice-start = ((s8[4718592]{0:T(1024)(128)(4,1)}), s8[4194304]{0:T(1024)(128)(4,1)S(1)}, s32[]{:S(2)}) async-start(s8[4718592]{0:T(1024)(128)(4,1)} %bitcast.92), calls=%async_computation.2 | async-start | bytes 8388608
  446.8 28.5 %slice-start.4 = ((s8[4718592]{0:T(1024)(128)(4,1)}), s8[4194304]{0:T(1024)(128)(4,1)S(1)}, s32[]{:S(2)}) async-start(s8[4718592]{0:T(1024)(128)(4,1)} %bitcast.98), calls=%async_computation.6 | async-start | bytes 8388608
  446.8 28.5 %slice-start.1 = ((s8[4718592]{0:T(1024)(128)(4,1)}), s8[524288]{0:T(1024)(128)(4,1)S(1)}, s32[]{:S(2)}) async-start(s8[4718592]{0:T(1024)(128)(4,1)} %bitcast.92), calls=%async_computation.3 | async-start | bytes 1048576
  446.8 28.5 %slice-start.5 = ((s8[4718592]{0:T(1024)(128)(4,1)}), s8[524288]{0:T(1024)(128)(4,1)S(1)}, s32[]{:S(2)}) async-start(s8[4718592]{0:T(1024)(128)(4,1)} %bitcast.98), calls=%async_computation.7 | async-start | bytes 1048576
  453.1 14.9 %collective-permute-start.8 = (bf16[1,1,1,2,1,24,3072]{6,5,4,3,2,1,0:T(8,128)(2,1)S(1)}, bf16[1,1,1,2,1,24,3072]{6,5,4,3,2,1,0:T(8,128)(2,1)S(1)}, u32[]{:S(2)}, u32[]{:S(2)}) collective-permute-start(bf16[1,1,1,2,1,24,3072]{6,5,4,3,2,1,0:T(8,128)(2,1)S(1)} %constant_dynamic-slice_fusion.15), channel_id=1, source_target_pairs={{0,16},{4,20},{8,24},{12,28},{16,0},{20,4},{24,8},{28,12},{1,17},{... | collective-permute-start | bytes 884744 | tf_op jit(solution)/shard_map/ppermute | solution.py:171
  468.1 5.8 collective-permute-start.9
  479.5 52.4 %collective-permute-start.21 = (bf16[2,2,2,1,1,192,768]{6,5,4,3,2,1,0:T(8,128)(2,1)S(1)}, bf16[2,2,2,1,1,192,768]{6,5,4,3,2,1,0:T(8,128)(2,1)S(1)}, u32[]{:S(2)}, u32[]{:S(2)}) collective-permute-start(bf16[2,2,2,1,1,192,768]{6,5,4,3,2,1,0:T(8,128)(2,1)S(1)} %constant_dynamic-slice_fusion.3), channel_id=1, source_target_pairs={{0,2},{1,3},{2,0},{3,1},{4,6},{5,7},{6,4},{7,5},{8,10},{9,11},{10,... | collective-permute-start | bytes 7077896 | tf_op jit(solution)/shard_map/ppermute | solution.py:171
  488.0 54.5 %collective-permute-start.11 = (bf16[2,2,1,2,1,24,6144]{6,5,4,3,2,1,0:T(8,128)(2,1)}, bf16[2,2,1,2,1,24,6144]{6,5,4,3,2,1,0:T(8,128)(2,1)}, u32[]{:S(2)}, u32[]{:S(2)}) collective-permute-start(bf16[2,2,1,2,1,24,6144]{6,5,4,3,2,1,0:T(8,128)(2,1)} %constant_dynamic-slice_fusion.12), channel_id=1, source_target_pairs={{0,4},{4,0},{8,12},{12,8},{16,20},{20,16},{24,28},{28,24},{1,5},{5... | collective-permute-start | bytes 7077896 | tf_op jit(solution)/shard_map/ppermute | solution.py:171
  495.3 66.9 %collective-permute-start.16 = (bf16[2,1,2,2,1,24,6144]{6,5,4,3,2,1,0:T(8,128)(2,1)S(1)}, bf16[2,1,2,2,1,24,6144]{6,5,4,3,2,1,0:T(8,128)(2,1)S(1)}, u32[]{:S(2)}, u32[]{:S(2)}) collective-permute-start(bf16[2,1,2,2,1,24,6144]{6,5,4,3,2,1,0:T(8,128)(2,1)S(1)} %constant_dynamic-slice_fusion.7), channel_id=1, source_target_pairs={{0,8},{4,12},{8,0},{12,4},{16,24},{20,28},{24,16},{28,20},{1,9},{5... | collective-permute-start | bytes 7077896 | tf_op jit(solution)/shard_map/ppermute | solution.py:171
  532.7 32.9 %collective-permute-start.22 = (bf16[2,2,1,1,1,192,768]{6,5,4,3,2,1,0:T(8,128)(2,1)S(1)}, bf16[2,2,1,1,1,192,768]{6,5,4,3,2,1,0:T(8,128)(2,1)S(1)}, u32[]{:S(2)}, u32[]{:S(2)}) collective-permute-start(bf16[2,2,1,1,1,192,768]{6,5,4,3,2,1,0:T(8,128)(2,1)S(1)} %constant_dynamic-slice_fusion.2), channel_id=1, source_target_pairs={{0,4},{4,0},{8,12},{12,8},{16,20},{20,16},{24,28},{28,24},{1,5},{5... | collective-permute-start | bytes 3538952 | tf_op jit(solution)/shard_map/ppermute | solution.py:171
  544.9 47.8 %collective-permute-start.12 = (bf16[2,1,1,2,1,24,6144]{6,5,4,3,2,1,0:T(8,128)(2,1)S(1)}, bf16[2,1,1,2,1,24,6144]{6,5,4,3,2,1,0:T(8,128)(2,1)S(1)}, u32[]{:S(2)}, u32[]{:S(2)}) collective-permute-start(bf16[2,1,1,2,1,24,6144]{6,5,4,3,2,1,0:T(8,128)(2,1)S(1)} %constant_dynamic-slice_fusion.11), channel_id=1, source_target_pairs={{0,8},{4,12},{8,0},{12,4},{16,24},{20,28},{24,16},{28,20},{1,9},{5... | collective-permute-start | bytes 3538952 | tf_op jit(solution)/shard_map/ppermute | solution.py:171
  563.1 65.7 %collective-permute-start.17 = (bf16[1,1,2,2,1,24,6144]{6,5,4,3,2,1,0:T(8,128)(2,1)S(1)}, bf16[1,1,2,2,1,24,6144]{6,5,4,3,2,1,0:T(8,128)(2,1)S(1)}, u32[]{:S(2)}, u32[]{:S(2)}) collective-permute-start(bf16[1,1,2,2,1,24,6144]{6,5,4,3,2,1,0:T(8,128)(2,1)S(1)} %constant_dynamic-slice_fusion.6), channel_id=1, source_target_pairs={{0,16},{4,20},{8,24},{12,28},{16,0},{20,4},{24,8},{28,12},{1,17},{... | collective-permute-start | bytes 3538952 | tf_op jit(solution)/shard_map/ppermute | solution.py:171
  565.9 63.8 %collective-permute-start.23 = (bf16[2,1,1,1,1,192,768]{6,5,4,3,2,1,0:T(8,128)(2,1)S(1)}, bf16[2,1,1,1,1,192,768]{6,5,4,3,2,1,0:T(8,128)(2,1)S(1)}, u32[]{:S(2)}, u32[]{:S(2)}) collective-permute-start(bf16[2,1,1,1,1,192,768]{6,5,4,3,2,1,0:T(8,128)(2,1)S(1)} %constant_dynamic-slice_fusion.1), channel_id=1, source_target_pairs={{0,8},{4,12},{8,0},{12,4},{16,24},{20,28},{24,16},{28,20},{1,9},{5... | collective-permute-start | bytes 1769480 | tf_op jit(solution)/shard_map/ppermute | solution.py:171
  593.0 47.4 %collective-permute-start.13 = (bf16[1,1,1,2,1,24,6144]{6,5,4,3,2,1,0:T(8,128)(2,1)S(1)}, bf16[1,1,1,2,1,24,6144]{6,5,4,3,2,1,0:T(8,128)(2,1)S(1)}, u32[]{:S(2)}, u32[]{:S(2)}) collective-permute-start(bf16[1,1,1,2,1,24,6144]{6,5,4,3,2,1,0:T(8,128)(2,1)S(1)} %constant_dynamic-slice_fusion.10), channel_id=1, source_target_pairs={{0,16},{4,20},{8,24},{12,28},{16,0},{20,4},{24,8},{28,12},{1,17},{... | collective-permute-start | bytes 1769480 | tf_op jit(solution)/shard_map/ppermute | solution.py:171
  629.2 12.0 %collective-permute-start.18 = (bf16[1,1,2,1,1,24,6144]{6,5,4,3,2,1,0:T(8,128)(2,1)S(1)}, bf16[1,1,2,1,1,24,6144]{6,5,4,3,2,1,0:T(8,128)(2,1)S(1)}, u32[]{:S(2)}, u32[]{:S(2)}) collective-permute-start(bf16[1,1,2,1,1,24,6144]{6,5,4,3,2,1,0:T(8,128)(2,1)S(1)} %constant_dynamic-slice_fusion.5), channel_id=1, source_target_pairs={{0,2},{1,3},{2,0},{3,1},{4,6},{5,7},{6,4},{7,5},{8,10},{9,11},{10,... | collective-permute-start | bytes 1769480 | tf_op jit(solution)/shard_map/ppermute | solution.py:171
  629.9 19.3 %collective-permute-start.24 = (bf16[1,1,1,1,1,192,768]{6,5,4,3,2,1,0:T(8,128)(2,1)S(1)}, bf16[1,1,1,1,1,192,768]{6,5,4,3,2,1,0:T(8,128)(2,1)S(1)}, u32[]{:S(2)}, u32[]{:S(2)}) collective-permute-start(bf16[1,1,1,1,1,192,768]{6,5,4,3,2,1,0:T(8,128)(2,1)S(1)} %constant_dynamic-slice_fusion), channel_id=1, source_target_pairs={{0,16},{4,20},{8,24},{12,28},{16,0},{20,4},{24,8},{28,12},{1,17},{... | collective-permute-start | bytes 884744 | tf_op jit(solution)/shard_map/ppermute | solution.py:171
  640.6 6.8 %collective-permute-start.14 = (bf16[1,1,1,1,1,24,6144]{6,5,4,3,2,1,0:T(8,128)(2,1)S(1)}, bf16[1,1,1,1,1,24,6144]{6,5,4,3,2,1,0:T(8,128)(2,1)S(1)}, u32[]{:S(2)}, u32[]{:S(2)}) collective-permute-start(bf16[1,1,1,1,1,24,6144]{6,5,4,3,2,1,0:T(8,128)(2,1)S(1)} %constant_dynamic-slice_fusion.9), channel_id=1, source_target_pairs={{0,2},{1,3},{2,0},{3,1},{4,6},{5,7},{6,4},{7,5},{8,10},{9,11},{10,... | collective-permute-start | bytes 884744 | tf_op jit(solution)/shard_map/ppermute | solution.py:171
  641.3 6.8 %collective-permute-start.19 = (bf16[1,1,1,1,1,24,6144]{6,5,4,3,2,1,0:T(8,128)(2,1)S(1)}, bf16[1,1,1,1,1,24,6144]{6,5,4,3,2,1,0:T(8,128)(2,1)S(1)}, u32[]{:S(2)}, u32[]{:S(2)}) collective-permute-start(bf16[1,1,1,1,1,24,6144]{6,5,4,3,2,1,0:T(8,128)(2,1)S(1)} %constant_dynamic-slice_fusion.4), channel_id=1, source_target_pairs={{0,4},{4,0},{8,12},{12,8},{16,20},{20,16},{24,28},{28,24},{1,5},{5... | collective-permute-start | bytes 884744 | tf_op jit(solution)/shard_map/ppermute | solution.py:171
  (16 other events, 29.2 us)
Sparse Core Ops, SparseCore 0:
  11.4 80.1 all-gather.2
  94.4 128.7 all-gather.4
